TPU v7x, 32 devices: a whole 2x2x4 slice. The times are simulated.
32 devices in a mesh: dp: 8 (over y, x, core), seq: 4 (over z).
Axes of the slice: x: 2, y: 2, z: 4, core: 2. Of those that a mesh axis runs over, the one named last changes fastest.
Arguments:
- tokens: bfloat16 [16, 640, 512], P('dp', 'seq'), may hold values from -6 to 6
- cotangent: bfloat16 [16, 640, 512], P('dp', 'seq'), may hold values from -6 to 6
- routes: int32 [2, 16, 640, 2], P(None, 'dp', 'seq'), may hold values from 0 to 3, all different within a row
- token_mask: int32 [16, 640], P('dp'), may hold values from 0 to 1, as said below
- ln1_gain: bfloat16 [2, 512], P(None, 'dp'), may hold values from 0.5 to 1.5
- ln1_bias: bfloat16 [2, 512], P(None, 'dp'), may hold values from -1.1953125 to 1.1953125
- qkv_weight: bfloat16 [2, 512, 1536], P(None, 'dp'), may hold values from -0.375 to 0.375
- out_weight: bfloat16 [2, 512, 512], P(None, 'dp'), may hold values from -1 to 1
- ln2_gain: bfloat16 [2, 512], P(None, 'dp'), may hold values from 0.5 to 1.5
- ln2_bias: bfloat16 [2, 512], P(None, 'dp'), may hold values from -1.1953125 to 1.1953125
- router_weight: bfloat16 [2, 512, 4], P(None, 'dp'), may hold values from -0.1875 to 0.1875
- expert_in: bfloat16 [2, 4, 512, 2048], P(None, None, 'dp'), may hold values from -0.25 to 0.25
- expert_out: bfloat16 [2, 4, 2048, 512], P(None, None, 'dp'), may hold values from -0.5 to 0.5
Outputs:
- output: bfloat16 [16, 640, 512], P('dp', 'seq')
- token_grad: float32 [16, 640, 512], P('dp', 'seq')
- ln1_gain_grad: float32 [2, 512], P(None, 'dp')
- ln1_bias_grad: float32 [2, 512], P(None, 'dp')
- qkv_weight_grad: float32 [2, 512, 1536], P(None, 'dp')
- out_weight_grad: float32 [2, 512, 512], P(None, 'dp')
- ln2_gain_grad: float32 [2, 512], P(None, 'dp')
- ln2_bias_grad: float32 [2, 512], P(None, 'dp')
- router_weight_grad: float32 [2, 512, 4], P(None, 'dp')
- expert_in_grad: float32 [2, 4, 512, 2048], P(None, None, 'dp')
- expert_out_grad: float32 [2, 4, 2048, 512], P(None, None, 'dp')
Inputs may be any that keep to these rules, and one draw needn't show every extreme that they name: `token_mask`: in each image the valid tokens (1) come first and the pads (0) after them; each image has 481 to 640 valid tokens. `routes`: the two experts of a token differ.
All inputs are finite; a program needn't handle non-finite values.
Results may differ from a plain program's by a relative error of at most 0.028.
Values may be sent and summed in bfloat16 or wider, within the bound.
A program may use at most 320 MiB of HBM per device.

v0:
```python
import itertools

import jax
import jax.numpy as jnp
from jax import lax
from jax.experimental import pallas as pl
from jax.experimental.pallas import tpu as pltpu
from jax.sharding import PartitionSpec as P

HEAD = 64
EPS = 1e-06
NEG = -1e30
F32 = jnp.float32
BF16 = jnp.bfloat16
MESH = pl.DeviceIdType.MESH
VMEM_LIMIT = 60 * 1024 * 1024
EXPERT_TICKS = ((0, 2, 1, 1, 1, 1, 1, 1), (1, 0, 1, 0), (1,), (1, 1, 0))
HEAD_TICKS = ((0, 1, 1, 1), (1,), (1,))
DENSE_TICKS = (5, 6, 14)
NT = ((1,), (1,))
TN = ((0,), (0,))


def normalize(values):
    center = values - jnp.mean(values, -1, keepdims=True)
    inverse = lax.rsqrt(jnp.mean(center * center, -1, keepdims=True) + EPS)
    return center * inverse, inverse


def norm_back(grad_unit, unit, inverse):
    return inverse * (
        grad_unit
        - jnp.mean(grad_unit, -1, keepdims=True)
        - unit * jnp.mean(grad_unit * unit, -1, keepdims=True)
    )


def in_vmem():
    return pl.BlockSpec(memory_space=pltpu.VMEM)


def in_any():
    return pl.BlockSpec(memory_space=pl.ANY)


def greet(*peers):
    barrier = pltpu.get_barrier_semaphore()
    count = 0
    for peer, condition in peers:

        def signal(peer=peer):
            pl.semaphore_signal(barrier, inc=1, device_id=peer, device_id_type=MESH)

        if condition is None:
            signal()
            count += 1
        else:
            pl.when(condition)(signal)
            count += condition.astype(jnp.int32)
    pl.semaphore_wait(barrier, count)


def remote(src, dst, send, recv, peer):
    return pltpu.make_async_remote_copy(
        src_ref=src, dst_ref=dst, send_sem=send, recv_sem=recv, device_id=peer, device_id_type=MESH
    )


def split_rows(rows8):
    high = rows8.astype(BF16).astype(F32)
    return jnp.concatenate([high, rows8 - high], 0).astype(BF16)


def join_rows(rows16):
    wide = rows16.astype(F32)
    return wide[:8] + wide[8:]


def gelu_parts(u):
    bell = jnp.exp2(u * u * -0.7213475204444817)
    t = pl.reciprocal(1.0 + 0.23164190 * jnp.abs(u), approx=True)
    poly = t * (
        0.127414796 + t * (-0.142248368 + t * (0.7107068705 + t * (-0.7265760135 + t * 0.5307027145)))
    )
    half = poly * bell
    cdf = jnp.where(u >= 0, 1.0 - half, half)
    return u * cdf, cdf + u * 0.3989422804014327 * bell


def dot(left, right, dims=((1,), (0,))):
    return lax.dot_general(left, right, (dims, ((), ())), preferred_element_type=F32)


def row_sums(values):
    return jnp.sum(values, 0, keepdims=True)


def pad_lanes(values, lanes):
    if values.shape[1] == lanes:
        return values
    return jnp.concatenate([values, jnp.zeros((values.shape[0], lanes - values.shape[1]), values.dtype)], 1)


def one_head(pair, parity):
    lane = lax.broadcasted_iota(jnp.int32, pair.shape, 1) // HEAD
    return jnp.where(lane == parity, pair.astype(F32), 0.0).astype(BF16)


def weight_rows(dense_ref):
    width = dense_ref.shape[0]
    return jnp.transpose(dense_ref[:, 4 * width :].astype(F32))


class Plan:
    def __init__(self, mesh, images, length):
        self.dp = mesh.shape["dp"]
        self.seq = mesh.shape["seq"]
        self.images = images
        self.piece = length // self.seq
        self.share = self.seq // images
        self.rows = images * self.piece


class Swap:
    def __init__(self, plan):
        self.plan = plan

    def where(self, k):
        me, mine = lax.axis_index("dp"), lax.axis_index("seq")
        share, images = self.plan.share, self.plan.images
        part = lax.rem(me, share)
        peer = {"dp": me - part + mine // images, "seq": part * images + k}
        stays = (part == mine // images) & (lax.rem(mine, images) == k)
        return peer, stays

    def peers(self):
        both = [self.where(k) for k in range(self.plan.images)]
        return [(peer, jnp.logical_not(stays)) for peer, stays in both]

    def start(self, src, dst, sems):
        slot = lax.rem(lax.axis_index("seq"), self.plan.images)
        for k in range(self.plan.images):
            peer, stays = self.where(k)

            @pl.when(jnp.logical_not(stays))
            def _():
                remote(src.at[k], dst.at[slot], sems.at[0, k], sems.at[1, slot], peer).start()

            @pl.when(stays)
            def _():
                pltpu.make_async_copy(src.at[k], dst.at[k], sems.at[1, k]).start()

    def wait(self, src, dst, sems):
        for k in range(self.plan.images):
            peer, stays = self.where(k)
            moved = remote(src.at[k], dst.at[k], sems.at[0, k], sems.at[1, k], peer)

            @pl.when(jnp.logical_not(stays))
            def _():
                moved.wait_recv()
                moved.wait_send()

            @pl.when(stays)
            def _():
                pltpu.make_async_copy(src.at[k], dst.at[k], sems.at[1, k]).wait()


class Slots:
    def __init__(self, ref):
        self.ref = ref
        self.rows = ref.shape[1]

    def at(self, slot, part, device):
        return self.ref.at[slot, part]


class Strips:
    def __init__(self, ref, rows):
        self.ref = ref
        self.rows = rows

    def at(self, slot, part, device):
        first = pl.multiple_of((device ^ slot) * self.rows + part.start, 16)
        return self.ref.at[pl.ds(first, part.size)]


class Spread:
    def __init__(self, size):
        self.size = size
        self.pairs = size // 2
        self.order = sorted(range(self.pairs), key=lambda pair: (bin(pair).count("1"), pair))
        self.bits = [1 << k for k in range(self.pairs.bit_length() - 1)]

    def ways(self, pair):
        return (pair & -pair, 1 << (pair.bit_length() - 1))

    def pair_at(self, turn):
        if isinstance(turn, int):
            return self.order[turn]
        pair = turn
        for at, value in enumerate(self.order):
            if at != value:
                pair = jnp.where(turn == at, value, pair)
        return pair

    def peers(self):
        me = lax.axis_index("dp")
        return [({"dp": me ^ r}, None) for r in (1, *range(2, self.size, 2))]

    def semaphores(self):
        return [
            pltpu.SemaphoreType.DMA((2, self.pairs)),
            pltpu.SemaphoreType.DMA((2, self.size)),
            pltpu.SemaphoreType.DMA((self.pairs,)),
        ]

    def bind(self, slots, semaphores):
        self.slots = slots
        self.send, self.recv, self.hand = semaphores
        self.me = lax.axis_index("dp")
        cut = slots.rows // 32 * 16
        self.whole = pl.ds(0, slots.rows)
        self.halves = (pl.ds(0, cut), pl.ds(cut, slots.rows - cut))

    def move(self, slot, to_slot, part, peer, send, recv):
        return remote(
            self.slots.at(slot, part, self.me), self.slots.at(to_slot, part, peer), send, recv, {"dp": peer}
        )

    def block(self, pair):
        slot = 2 * pair
        return self.move(0, slot, self.whole, self.me ^ slot, self.send.at[0, pair], self.recv.at[0, slot])

    def half_block(self, pair, half):
        way = self.ways(pair)[half]
        return self.move(
            2 * (pair ^ way), 2 * pair, self.halves[half], self.me ^ (2 * way),
            self.send.at[half, pair], self.recv.at[half, 2 * pair],
        )

    def handed(self, pair):
        slot = 2 * pair
        return self.move(
            slot, slot + 1, self.whole, self.me ^ 1, self.hand.at[pair], self.recv.at[0, slot + 1]
        )

    def start(self):
        self.handed(0).start()
        for bit in self.bits:
            self.block(bit).start()

    def arrive(self, pair):
        for known in range(1, self.pairs):

            @pl.when(jnp.asarray(pair) == known)
            def _():
                if known in self.bits:
                    self.block(known).wait_recv()
                else:
                    self.half_block(known, 0).wait_recv()
                    self.half_block(known, 1).wait_recv()
                for far in range(1, self.pairs):
                    for half, way in enumerate(self.ways(far)):
                        if far not in self.bits and far ^ way == known:
                            self.half_block(far, half).start()

        self.handed(pair).start()

    def drain(self):
        for pair in range(self.pairs):
            self.handed(pair).wait_send()
            if pair in self.bits:
                self.block(pair).wait_send()
            elif pair:
                self.half_block(pair, 0).wait_send()
                self.half_block(pair, 1).wait_send()


class Group(Spread):
    def scratch(self, rows, tail, width):
        full = rows + tail
        return self.semaphores() + [
            pltpu.VMEM((self.pairs, rows, width), F32),
            pltpu.VMEM((self.pairs, 8, width), F32),
            pltpu.VMEM((self.pairs, full, width), BF16),
            pltpu.VMEM((self.pairs, full, width), BF16),
            pltpu.VMEM((self.pairs, full, width), BF16),
            pltpu.VMEM((self.pairs, full, width), BF16),
            pltpu.SemaphoreType.DMA((self.pairs,)),
            pltpu.SemaphoreType.DMA((self.pairs,)),
            pltpu.SemaphoreType.DMA((self.pairs,)),
            pltpu.SemaphoreType.DMA((self.pairs,)),
        ]

    def given(self, pair):
        return remote(
            self.give.at[pair], self.take.at[pair], self.g_send.at[pair], self.g_recv.at[pair], {"dp": self.me ^ 1}
        )

    def paid(self, pair):
        return remote(
            self.pay.at[pair], self.due.at[pair], self.p_send.at[pair], self.p_recv.at[pair],
            {"dp": self.me ^ (2 * pair)},
        )

    def run(self, slots, scratch, rows, tail, compute):
        self.bind(Slots(slots), scratch[:3])
        (
            self.own, self.own_tail, self.give, self.take, self.pay, self.due,
            self.g_send, self.g_recv, self.p_send, self.p_recv,
        ) = scratch[3:]
        self.sizes = rows, tail

        def settle(pair):
            self.given(pair).wait_recv()
            self.own[pair] += self.take[pair, :rows].astype(F32)
            if tail:
                self.own_tail[pair] += join_rows(self.take[pair, rows:])

            @pl.when(jnp.asarray(pair) > 0)
            def _():
                self.pay[pair, :rows] = self.own[pair].astype(BF16)
                if tail:
                    self.pay[pair, rows:] = split_rows(self.own_tail[pair])
                self.paid(pair).start()

        self.start()

        def step(at, carry):
            turn = at // 2
            pair = self.pair_at(turn)
            even = lax.rem(at, 2) == 0
            slot = 2 * pair + lax.rem(at, 2)

            @pl.when(even & (turn > 0))
            def _():
                self.arrive(pair)
                settle(self.pair_at(turn - 1))

            @pl.when(jnp.logical_not(even))
            def _():
                self.handed(pair).wait_recv()

            total, total_tail = compute(slot, at)

            @pl.when(even)
            def _():
                self.own[pair] = total
                if tail:
                    self.own_tail[pair] = total_tail

            @pl.when(jnp.logical_not(even))
            def _():
                self.give[pair, :rows] = total.astype(BF16)
                if tail:
                    self.give[pair, rows:] = split_rows(total_tail)
                self.given(pair).start()

            return carry

        lax.fori_loop(0, self.size, step, 0)
        settle(self.order[-1])

    def collect(self, between=()):
        rows, tail = self.sizes
        for pair, steps in zip(self.order[1:], itertools.chain(between, itertools.repeat(()))):
            self.paid(pair).wait_recv()
            for step in steps:
                step()
            self.own[0] += self.due[pair, :rows].astype(F32)
            if tail:
                self.own_tail[0] += join_rows(self.due[pair, rows:])
        for pair in range(self.pairs):
            self.given(pair).wait_send()
            if pair:
                self.paid(pair).wait_send()
        self.drain()


def experts_forward(message, middle, up, down, size, strip=None):
    rows, width = middle.shape
    experts, _, hid = up.shape
    wide = experts * hid
    group = Group(size)
    spread = Spread(size)
    extra = [] if strip is None else [strip]

    def kernel(msg_ref, mid_ref, up_ref, down_ref, *refs):
        strip_ref, refs = refs[: len(extra)], refs[len(extra) :]
        (out_ref, low_ref, all_ref, act_ref, slope_ref), refs = refs[:5], refs[5:]
        dense_ref, refs = refs[: len(extra)], refs[len(extra) :]
        (slots, act, slope, scaled, save_sem), refs = refs[:5], refs[5:]
        scratch, refs = refs[:13], refs[13:]
        if extra:
            dense_all, keep_sem, *sems = refs
            me = lax.axis_index("dp")
            spread.bind(Strips(dense_all, strip.shape[0]), sems)
            dense_all[pl.ds(pl.multiple_of(me * strip.shape[0], 16), strip.shape[0])] = strip_ref[0][...]
        greet(*group.peers())
        slots[0] = msg_ref[...]

        def saves(slot):
            return (
                pltpu.make_async_copy(slots.at[slot], all_ref.at[slot], save_sem.at[slot, 0]),
                pltpu.make_async_copy(act.at[slot], act_ref.at[slot], save_sem.at[slot, 1]),
                pltpu.make_async_copy(slope.at[slot], slope_ref.at[slot], save_sem.at[slot, 2]),
            )

        def compute(slot, at):
            gates = jnp.transpose(join_rows(slots[slot, rows:]))[:rows]
            for expert in range(experts):
                cols = slice(expert * hid, (expert + 1) * hid)
                value, grade = gelu_parts(dot(slots[slot, :rows], up_ref[expert]))
                value = value.astype(BF16)
                act[slot, :, cols] = value
                slope[slot, :, cols] = grade.astype(BF16)
                scaled[:, cols] = (value.astype(F32) * gates[:, expert : expert + 1]).astype(BF16)
            for save in saves(slot):
                save.start()
            if extra:
                pl.when(at == 0)(spread.start)
                for turn, pair in enumerate(spread.order[1:], 1):
                    pl.when(at == (3 if pair in spread.bits else 5))(lambda pair=pair: spread.arrive(pair))
            return dot(scaled[...], down_ref[...]), None

        group.run(slots, scratch, rows, 0, compute)
        if extra:
            for pair in spread.order:
                spread.handed(pair).wait_recv()
            keep = pltpu.make_async_copy(dense_all, dense_ref[0], keep_sem)
            keep.start()
        group.collect()
        out = mid_ref[...] + group.own[0]
        out_ref[...] = out
        low_ref[...] = out.astype(BF16)
        for slot in range(size):
            for save in saves(slot):
                save.wait()
        if extra:
            spread.drain()
            keep.wait()

    return pl.pallas_call(
        kernel,
        out_shape=(
            jax.ShapeDtypeStruct((rows, width), F32),
            jax.ShapeDtypeStruct((rows, width), BF16),
            jax.ShapeDtypeStruct((size, rows + 16, width), BF16),
            jax.ShapeDtypeStruct((size, rows, wide), BF16),
            jax.ShapeDtypeStruct((size, rows, wide), BF16),
            *[jax.ShapeDtypeStruct((size * item.shape[0], item.shape[1]), BF16) for item in extra],
        ),
        in_specs=[in_vmem()] * (4 + len(extra)),
        out_specs=(in_vmem(), in_vmem(), in_any(), in_any(), in_any()) + (in_any(),) * len(extra),
        scratch_shapes=[
            pltpu.VMEM((size, rows + 16, width), BF16),
            pltpu.VMEM((size, rows, wide), BF16),
            pltpu.VMEM((size, rows, wide), BF16),
            pltpu.VMEM((rows, wide), BF16),
            pltpu.SemaphoreType.DMA((size, 3)),
        ]
        + group.scratch(rows, 0, width)
        + (
            [pltpu.VMEM((size * strip.shape[0], strip.shape[1]), BF16), pltpu.SemaphoreType.DMA]
            + spread.semaphores()
            if extra
            else []
        ),
        compiler_params=pltpu.CompilerParams(
            collective_id=10 if extra else 1, has_side_effects=True, vmem_limit_bytes=VMEM_LIMIT
        ),
        name="experts_forward",
    )(message, middle, up, down, *extra)


class Shift:
    def __init__(self, source):
        experts, self.dp, quarters, r, self.hid = source.shape
        self.experts = experts
        self.shape = (experts, quarters, r, self.dp * self.hid)
        self.scratch_shapes = [
            pltpu.VMEM(self.shape, BF16),
            pltpu.VMEM((self.dp, experts, quarters, r, self.hid), BF16),
            pltpu.SemaphoreType.DMA((2, self.dp)),
        ]

    def copy(self, src, dst, box, sems, r):
        me = lax.axis_index("dp")
        return remote(src.at[:, me ^ r], box.at[me], sems.at[0, r], sems.at[1, r], {"dp": me ^ r})

    def start(self, *refs):
        for r in range(1, self.dp):
            self.copy(*refs, r).start()

    def arrive(self, src, dst, box, sems):
        me = lax.axis_index("dp")
        box[me] = src[:, me]
        for r in range(1, self.dp):
            self.copy(src, dst, box, sems, r).wait_recv()
        for owner in range(self.dp):
            dst[:, :, :, owner * self.hid : (owner + 1) * self.hid] = box[owner]

    def drain(self, *refs):
        for r in range(1, self.dp):
            self.copy(*refs, r).wait_send()


class LineSums:
    def __init__(self, dp=0, down_chunks=None, **arrays):
        self.dp = dp
        self.first = down_chunks[0] if down_chunks else 0
        self.kinds = list(arrays)
        self.args = tuple(array for array in arrays.values() if not isinstance(array, jax.ShapeDtypeStruct))
        self.dense = [kind for kind in self.kinds if kind.startswith("dense")]
        self.chunk, self.count = {}, {}
        self.out_shape, self.scratch_shapes = (), []
        for kind, array in arrays.items():
            shape = array.shape
            special = []
            if kind == "up":
                self.chunk[kind], self.count[kind] = shape[2:], shape[0] * shape[1]
            elif kind == "down":
                self.chunk[kind] = shape[1:]
                self.count[kind] = down_chunks[1] - down_chunks[0] if down_chunks else shape[0]
            else:
                self.chunk[kind], self.count[kind] = (shape[2] // 4, shape[3]), 4
                whole = (dp // 2,) + shape[2:]
                special = [
                    pltpu.VMEM(whole, BF16),
                    pltpu.VMEM(whole, BF16),
                    pltpu.VMEM((4,) + self.chunk[kind], BF16),
                    pltpu.SemaphoreType.DMA((2,)),
                    pltpu.SemaphoreType.DMA((2, dp // 2)),
                ]
            count, chunk = self.count[kind], self.chunk[kind]
            self.out_shape += (jax.ShapeDtypeStruct((count,) + chunk, BF16),)
            self.scratch_shapes += [
                pltpu.VMEM((count,) + chunk, BF16),
                pltpu.VMEM((count // 2,) + chunk, BF16),
                pltpu.VMEM((count // 2,) + chunk, BF16),
                pltpu.VMEM((count,) + chunk, BF16),
                pltpu.SemaphoreType.DMA((2, count)),
                pltpu.SemaphoreType.DMA((2, count // 2)),
                pltpu.SemaphoreType.DMA((2, count)),
                pltpu.SemaphoreType.DMA((count // 2,)),
                pltpu.SemaphoreType.DMA,
            ] + special
        self.pairs = [(kind, p) for kind in self.kinds for p in range(self.count[kind] // 2)]

    def peers(self):
        if not self.kinds:
            return []
        mine = lax.axis_index("seq")
        middle = (mine == 1) | (mine == 2)
        return [
            ({"seq": jnp.where(middle, 3 - mine, 1 + mine // 2)}, None),
            ({"seq": jnp.where(middle, 3 * (mine - 1), mine)}, middle),
        ]

    def bind(self, refs, outs, scratch):
        self.refs = dict(zip(self.kinds, refs))
        self.outs = dict(zip(self.kinds, outs))
        self.boxes = {}
        for kind in self.kinds:
            held = 14 if kind in self.dense else 9
            self.boxes[kind], scratch = scratch[:held], scratch[held:]
        self.me, self.mine = lax.axis_index("dp"), lax.axis_index("seq")
        self.middle = (self.mine == 1) | (self.mine == 2)
        self.inner = {"seq": jnp.where(self.middle, 3 - self.mine, 1 + self.mine // 2)}
        self.outer = {"seq": jnp.where(self.middle, 3 * (self.mine - 1), self.mine)}
        self.side = jnp.where(self.mine == 2, 1, 0)

    def source(self, kind, c):
        if kind == "up":
            return self.refs[kind].at[c // 4, lax.rem(c, 4)]
        return self.boxes[kind][11].at[c] if kind in self.dense else self.refs[kind].at[self.first + c]

    def inward(self, kind, c):
        box, sem = self.boxes[kind][0], self.boxes[kind][4]
        return remote(self.source(kind, c), box.at[c], sem.at[0, c], sem.at[1, c], self.inner)

    def across(self, kind, p):
        box, sem = self.boxes[kind], self.boxes[kind][5]
        return remote(box[2].at[p], box[1].at[p], sem.at[0, p], sem.at[1, p], self.inner)

    def outward(self, kind, c):
        box, sem = self.boxes[kind][3], self.boxes[kind][6]
        return remote(box.at[c], box.at[c], sem.at[0, c], sem.at[1, c], self.outer)

    def between(self, kind, c, p):
        box = self.boxes[kind]
        return remote(box[3].at[c], box[3].at[c], box[7].at[p], box[6].at[1, c], self.inner)

    def near_copy(self, kind):
        box = self.boxes[kind]
        away = self.refs[kind].at[:, 1 - lax.rem(self.me, 2)]
        return remote(away, box[9], box[12].at[0], box[12].at[1], {"dp": self.me ^ 1})

    def far(self, kind, m):
        box = self.boxes[kind]
        return remote(
            box[9].at[(self.me // 2) ^ m], box[10].at[m], box[13].at[0, m], box[13].at[1, m],
            {"dp": self.me ^ (2 * m)},
        )

    def begin(self, *kinds):
        @pl.when(jnp.logical_not(self.middle))
        def _():
            for kind in kinds:
                for c in range(self.count[kind]):
                    self.inward(kind, c).start()

    def dense_begin(self, kind):
        self.near_copy(kind).start()

    def dense_near(self, kind):
        self.near_copy(kind).wait_recv()
        box = self.boxes[kind]
        for at in range(self.dp // 2):
            box[9][at] = (
                self.refs[kind][at, lax.rem(self.me, 2)].astype(F32) + box[9][at].astype(F32)
            ).astype(BF16)
        for m in range(1, self.dp // 2):
            self.far(kind, m).start()

    def dense_far(self, kind):
        for m in range(1, self.dp // 2):
            self.far(kind, m).wait_recv()
        box = self.boxes[kind]
        rows = self.chunk[kind][0]
        for at in range(4):
            place = slice(at * rows, (at + 1) * rows)
            total = box[9][self.me // 2, place].astype(F32)
            for m in range(1, self.dp // 2):
                total += box[10][m, place].astype(F32)
            box[11][at] = total.astype(BF16)
        self.begin(kind)

    def relay(self, kind, p):
        c = 2 * p + 1 - self.side
        box = self.boxes[kind]
        self.inward(kind, c).wait_recv()
        box[2][p] = (self.source(kind, c)[...].astype(F32) + box[0][c].astype(F32)).astype(BF16)
        self.across(kind, p).start()

    def total(self, kind, p):
        c = 2 * p + self.side
        box = self.boxes[kind]
        self.inward(kind, c).wait_recv()
        self.across(kind, p).wait_recv()
        box[3][c] = (
            self.source(kind, c)[...].astype(F32) + box[0][c].astype(F32) + box[1][p].astype(F32)
        ).astype(BF16)
        self.between(kind, c, p).start()
        self.outward(kind, c).start()

    def forward(self, kind, p):
        c = 2 * p + 1 - self.side
        self.outward(kind, c).wait_recv()
        self.outward(kind, c).start()

    def ticks(self):
        count = len(self.pairs)
        if not count:
            return []

        def tick(at):
            @pl.when(self.middle)
            def _():
                for act, behind in ((self.relay, 0), (self.total, 1), (self.forward, 2)):
                    if 0 <= at - behind < count:
                        act(*self.pairs[at - behind])

        return [lambda at=at: tick(at) for at in range(count + 2)]

    def share_out(self, places):
        ticks, shared = self.ticks(), []
        for counts in places:
            group = []
            for count in counts:
                group.append(ticks[:count])
                ticks = ticks[count:]
            shared.append(group)
        return (*shared, ticks)

    def finish(self):
        if not self.kinds:
            return

        @pl.when(jnp.logical_not(self.middle))
        def _():
            for kind in self.kinds:
                for c in range(self.count[kind]):
                    self.outward(kind, c).wait_recv()
                    self.inward(kind, c).wait_send()

        copies = [
            pltpu.make_async_copy(self.boxes[kind][3], self.outs[kind], self.boxes[kind][8]) for kind in self.kinds
        ]
        for copy in copies:
            copy.start()

        @pl.when(self.middle)
        def _():
            for kind, p in self.pairs:
                self.across(kind, p).wait_send()
                self.between(kind, 2 * p + self.side, p).wait_send()
                self.outward(kind, 2 * p).wait_send()
                self.outward(kind, 2 * p + 1).wait_send()

        for kind in self.dense:
            self.near_copy(kind).wait_send()
            for m in range(1, self.dp // 2):
                self.far(kind, m).wait_send()
        for copy in copies:
            copy.wait()


def sum_weights_plainly(dp, down, up, dense):
    dense = lax.psum_scatter(dense.reshape(dp, -1, dense.shape[-1]), "dp", scatter_dimension=0, tiled=True)
    up = lax.all_to_all(up, "dp", split_axis=1, concat_axis=1, tiled=True)
    experts, _, quarters, r, hid = up.shape
    up = jnp.transpose(up.reshape(experts, dp, quarters * r, hid), (0, 2, 1, 3))
    return lax.psum(down, "seq"), lax.psum(up.reshape(experts, quarters * r, -1), "seq"), lax.psum(dense, "seq")


def experts_backward(grad, blocks, act, slope, up, down, plan, job, leaving=None):
    rows, width = grad.shape
    experts, _, hid = up.shape
    wide = experts * hid
    size = plan.dp
    group = Group(size)
    swap = Swap(plan)
    extra = [] if leaving is None else [leaving]

    def kernel(*refs):
        (grad_ref, blocks_ref, act_ref, slope_ref, up_ref, down_ref), refs = refs[:6], refs[6:]
        if extra:
            leaving_ref, refs = refs[0], refs[1:]
        job_refs, refs = refs[: len(job.args)], refs[len(job.args) :]
        (out_ref, tail_ref, up_out, down_out), refs = refs[:4], refs[4:]
        if extra:
            left_ref, refs = refs[0], refs[1:]
        job_outs, refs = refs[: len(job.args)], refs[len(job.args) :]
        slots, blocks, facts, act, slope, weighed, scaled, pre, flat, load_sem = refs[:10]
        refs = refs[10:]
        scratch, refs = refs[:13], refs[13:]
        if extra:
            (left, left_sem), refs = refs[:2], refs[2:]
        job.bind(job_refs, job_outs, refs)
        in_steps, in_sums, before, between, rest = job.share_out(EXPERT_TICKS)

        def loads(at):
            two = lax.rem(at, 2)
            slot = 2 * group.pair_at(at // 2) + two
            place = pl.ds(pl.multiple_of(slot * rows, 16), rows)
            return (
                pltpu.make_async_copy(blocks_ref.at[slot, pl.ds(0, rows)], blocks.at[place], load_sem.at[two, 0]),
                pltpu.make_async_copy(act_ref.at[slot], act.at[two], load_sem.at[two, 1]),
                pltpu.make_async_copy(slope_ref.at[slot], slope.at[two], load_sem.at[two, 2]),
                pltpu.make_async_copy(blocks_ref.at[slot, pl.ds(rows, 16)], facts.at[two], load_sem.at[two, 3]),
            )

        for load in loads(0):
            load.start()
        greet(*group.peers(), *job.peers(), *(swap.peers() if extra else []))
        slots[0] = grad_ref[...]
        if extra:
            swap.start(leaving_ref, left, left_sem)
        for expert in range(experts):
            flat[:, expert * hid : (expert + 1) * hid] = up_ref[expert]
        lane = lax.broadcasted_iota(jnp.int32, (16, wide), 1) // hid
        pick = (lane == lax.broadcasted_iota(jnp.int32, (16, wide), 0)).astype(F32).astype(BF16)

        def compute(slot, at):
            two = lax.rem(at, 2)

            @pl.when(at + 1 < size)
            def _():
                for load in loads(at + 1):
                    load.start()

            for load in loads(at):
                load.wait()
            gates = jnp.transpose(join_rows(facts[two]))[:rows]
            place = pl.ds(pl.multiple_of(slot * rows, 16), rows)
            for expert in range(experts):
                cols = slice(expert * hid, (expert + 1) * hid)
                gate = gates[:, expert : expert + 1]
                pull = dot(slots[slot], down_ref[cols, :], NT)
                value = act[two, :, cols].astype(F32)
                weighed[:, cols] = (pull * value).astype(BF16)
                scaled[place, cols] = (value * gate).astype(BF16)
                pre[place, cols] = (pull * gate * slope[two, :, cols].astype(F32)).astype(BF16)
            if job.kinds:
                pl.when(at == 0)(lambda: job.begin(*job.kinds))
                for step, ticks in enumerate(in_steps):
                    for tick in ticks:
                        pl.when(at == step)(tick)
            by_expert = pad_lanes(dot(pick, weighed[...], NT)[:8], width)
            return dot(pre[place, :], flat[...], NT), by_expert

        group.run(slots, scratch, rows, 16, compute)

        def weight_sums(expert, carry):
            cols = pl.ds(pl.multiple_of(expert * hid, 128), hid)
            down_out[cols, :] = dot(scaled[:, cols], slots[...].reshape(size * rows, width), TN).astype(BF16)
            up_out[expert] = dot(blocks[...], pre[:, cols], TN).astype(BF16)
            for step, ticks in enumerate(in_sums):
                for tick in ticks:
                    pl.when(expert == step)(tick)
            return carry

        lax.fori_loop(0, experts, weight_sums, 0)
        for tick in before[0]:
            tick()
        group.collect(between)
        out_ref[...] = group.own[0]
        tail_ref[...] = group.own_tail[0]
        for tick in rest:
            tick()
        job.finish()
        if extra:
            swap.wait(leaving_ref, left, left_sem)
            left_ref[...] = left[...]

    left_shape = [] if leaving is None else [jax.ShapeDtypeStruct(leaving.shape, BF16)]
    left_scratch = [
        pltpu.VMEM((plan.images, plan.piece, width), BF16),
        pltpu.SemaphoreType.DMA((2, plan.images)),
    ]
    return pl.pallas_call(
        kernel,
        out_shape=(
            jax.ShapeDtypeStruct((rows, width), F32),
            jax.ShapeDtypeStruct((8, width), F32),
            jax.ShapeDtypeStruct((experts, width, hid), BF16),
            jax.ShapeDtypeStruct((wide, width), BF16),
            *left_shape,
            *job.out_shape,
        ),
        in_specs=[in_vmem(), in_any(), in_any(), in_any(), in_vmem(), in_vmem()]
        + [in_vmem()] * (len(extra) + len(job.args)),
        out_specs=(in_vmem(),) * (4 + len(extra)) + (in_any(),) * len(job.args),
        scratch_shapes=[
            pltpu.VMEM((size, rows, width), BF16),
            pltpu.VMEM((size * rows, width), BF16),
            pltpu.VMEM((2, 16, width), BF16),
            pltpu.VMEM((2, rows, wide), BF16),
            pltpu.VMEM((2, rows, wide), BF16),
            pltpu.VMEM((rows, wide), BF16),
            pltpu.VMEM((size * rows, wide), BF16),
            pltpu.VMEM((size * rows, wide), BF16),
            pltpu.VMEM((width, wide), BF16),
            pltpu.SemaphoreType.DMA((2, 4)),
        ]
        + group.scratch(rows, 16, width)
        + (left_scratch if extra else [])
        + job.scratch_shapes,
        compiler_params=pltpu.CompilerParams(
            collective_id=3 if job.kinds else 2, has_side_effects=True, vmem_limit_bytes=VMEM_LIMIT
        ),
        name="experts_backward_and_sums" if job.kinds else "experts_backward",
    )(grad, blocks, act, slope, up, down, *extra, *job.args)


def attention_forward(plan, level, expert_in, later=None, entry=None):
    first = entry is not None
    share, size, rows = plan.share, plan.dp, plan.rows
    swap = Swap(plan)
    levels, experts, strip, hidden = expert_in.shape
    spread = Spread(size)
    width = strip * size
    columns = (entry or later)[1 + first].shape[-1]
    keys_len = rows * share
    heads = width // HEAD
    hid = hidden // size

    def kernel(in_ref, *refs):
        taken, refs = refs[:4], refs[4:]
        (message, middle, queries, kv, log_total, mixed, gates_ref, up_ref), refs = refs[:8], refs[8:]
        if first:
            (grad, grad_low, state_ref, chosen_all, length_ref, dense_out), refs = refs[:6], refs[6:]
        (all_kv, values_t, up_all, whole, parts, send, recv, save, up_send, up_recv), refs = refs[:10], refs[10:]
        bring = pltpu.make_async_copy(in_ref.at[level], whole, save)
        bring.start()
        me = lax.axis_index("dp")
        part = lax.rem(me, share)
        greet(*[({"dp": me ^ r}, None) for r in range(1, size)], *(swap.peers() if first else []))

        def shift(r):
            return remote(
                parts.at[me ^ r], up_all.at[:, pl.ds(pl.multiple_of(me * strip, 16), strip)],
                up_send.at[r], up_recv.at[r], {"dp": me ^ r},
            )

        if first:
            tokens_ref, facts_ref, dense_ref, cot_ref = taken
            tok, fact, cot, dense_all, tok_sem, fact_sem, cot_sem, keep_sem, *sems = refs
            dense_all[pl.ds(pl.multiple_of(me * strip, 16), strip)] = dense_ref[...]
            spread.bind(Strips(dense_all, strip), sems)
            spread.start()
            swap.start(facts_ref, fact, fact_sem)
            swap.start(tokens_ref, tok, tok_sem)
        bring.wait()
        for owner in range(size):
            parts[owner] = whole[:, :, owner * hid : (owner + 1) * hid]
        up_all[:, pl.ds(pl.multiple_of(me * strip, 16), strip)] = parts[me]
        if first:
            for pair in spread.order[1:]:
                spread.arrive(pair)
            for r in range(1, size):
                shift(r).start()
            swap.start(cot_ref, cot, cot_sem)
            swap.wait(facts_ref, fact, fact_sem)
            total = fact[0].astype(F32)
            for k in range(1, plan.images):
                total += fact[k].astype(F32)
            for at in range(levels):
                chosen_all[at] = total[8 * at : 8 * at + 8]
            length = total[8 * levels : 8 * levels + 1, :1] * 4.0 + total[8 * levels + 1 : 8 * levels + 2, :1]
            length_ref[...] = jnp.broadcast_to(length, length_ref.shape)
            swap.wait(tokens_ref, tok, tok_sem)
            for k in range(plan.images):
                state_ref[k * plan.piece : (k + 1) * plan.piece] = tok[k].astype(F32)
            for pair in spread.order:
                spread.handed(pair).wait_recv()
            keep_dense = pltpu.make_async_copy(dense_all, dense_out, keep_sem)
            keep_dense.start()
            dense_ref, chosen_ref = dense_all, chosen_all.at[level]
        else:
            state_ref, dense_ref, chosen_ref, length_ref = taken
            for r in range(1, size):
                shift(r).start()
        rows_of = weight_rows(dense_ref)
        unit, _ = normalize(state_ref[...])
        normed = (unit * rows_of[0:1] + rows_of[1:2]).astype(BF16)
        all_kv[part] = dot(normed, dense_ref[:, width : 3 * width]).astype(BF16)
        copies = [
            remote(all_kv.at[part], all_kv.at[part], send.at[k], recv.at[k], {"dp": me ^ k})
            for k in range(1, share)
        ]
        for copy in copies:
            copy.start()
        queries[...] = (dot(normed, dense_ref[:, :width]) * HEAD ** (-0.5)).astype(BF16)
        for copy in copies:
            copy.wait()
        saving = pltpu.make_async_copy(all_kv, kv, save)
        saving.start()
        for at in range(share):
            values_t[:, at * rows : (at + 1) * rows] = jnp.transpose(
                all_kv[at, :, width:].astype(F32)
            ).astype(BF16)
        key = lax.broadcasted_iota(jnp.int32, (keys_len, rows), 0)
        valid = key.astype(F32) < length_ref[0:1, 0:1]

        def pair_of_heads(pair, carry):
            lanes = pl.ds(pl.multiple_of(pair * 128, 128), 128)
            keys_pair = all_kv[:, :, lanes].reshape(keys_len, 128)
            queries_pair = queries[:, lanes]
            for parity in range(2):
                head = 2 * pair + parity
                scores = dot(keys_pair, one_head(queries_pair, parity), NT)
                scores = jnp.where(valid, scores, NEG)
                highest = jnp.max(scores, 0, keepdims=True)
                expo = jnp.exp(scores - highest)
                totals = row_sums(expo)
                log_total[head] = highest + jnp.log(totals)
                place = pl.ds(pl.multiple_of(head * HEAD, HEAD), HEAD)
                mixed[place, :] = (dot(values_t[place, :], expo.astype(BF16)) / totals).astype(BF16)
            return carry

        lax.fori_loop(0, heads // 2, pair_of_heads, 0)
        middle[...] = state_ref[...] + dot(mixed[...], dense_ref[:, 3 * width : 4 * width], TN)
        unit, _ = normalize(middle[...])
        normed = (unit * rows_of[2:3] + rows_of[3:4]).astype(BF16)
        message[:rows] = normed
        router = jnp.concatenate([rows_of[4:8], jnp.zeros((12, width), F32)], 0).astype(BF16)
        logits = dot(router, normed, NT)[:8]
        row = lax.broadcasted_iota(jnp.int32, logits.shape, 0)
        logits = jnp.where(row < experts, logits, NEG)
        expo = jnp.exp(logits - jnp.max(logits, 0, keepdims=True))
        gates = expo / row_sums(expo)
        gates_ref[...] = gates
        message[rows:] = split_rows(pad_lanes(gates * chosen_ref[:, :rows], width))
        saving.wait()
        for r in range(1, size):
            shift(r).wait_recv()
        keep = pltpu.make_async_copy(up_all, up_ref, save)
        keep.start()
        if first:
            swap.wait(cot_ref, cot, cot_sem)
            for k in range(plan.images):
                place = slice(k * plan.piece, (k + 1) * plan.piece)
                row = lax.broadcasted_iota(jnp.int32, (plan.piece, width), 0) + part * rows + k * plan.piece
                masked = jnp.where(row.astype(F32) < length_ref[0:1, 0:1], cot[k].astype(F32), 0.0)
                grad[place] = masked
                grad_low[place] = masked.astype(BF16)
            spread.drain()
            keep_dense.wait()
        for r in range(1, size):
            shift(r).wait_send()
        keep.wait()

    pieces = pltpu.VMEM((plan.images, plan.piece, width), BF16)
    swap_sem = pltpu.SemaphoreType.DMA((2, plan.images))
    entry_out, entry_specs, entry_scratch = (), (), []
    if first:
        entry_out = (
            jax.ShapeDtypeStruct((rows, width), F32),
            jax.ShapeDtypeStruct((rows, width), BF16),
            jax.ShapeDtypeStruct((rows, width), F32),
            jax.ShapeDtypeStruct((levels, 8, width), F32),
            jax.ShapeDtypeStruct((8, 128), F32),
            jax.ShapeDtypeStruct((width, columns), BF16),
        )
        entry_specs = (in_vmem(),) * 5 + (in_any(),)
        entry_scratch = [
            pieces,
            pltpu.VMEM(entry[1].shape, BF16),
            pieces,
            pltpu.VMEM((width, columns), BF16),
            swap_sem,
            swap_sem,
            swap_sem,
            pltpu.SemaphoreType.DMA,
        ] + spread.semaphores()
    return pl.pallas_call(
        kernel,
        out_shape=(
            jax.ShapeDtypeStruct((rows + 16, width), BF16),
            jax.ShapeDtypeStruct((rows, width), F32),
            jax.ShapeDtypeStruct((rows, width), BF16),
            jax.ShapeDtypeStruct((share, rows, 2 * width), BF16),
            jax.ShapeDtypeStruct((heads, 1, rows), F32),
            jax.ShapeDtypeStruct((width, rows), BF16),
            jax.ShapeDtypeStruct((8, rows), F32),
            jax.ShapeDtypeStruct((experts, width, hid), BF16),
            *entry_out,
        ),
        in_specs=[in_any()] + [in_vmem()] * 4,
        out_specs=(in_vmem(),) * 3 + (in_any(),) + (in_vmem(),) * 3 + (in_any(),) + entry_specs,
        scratch_shapes=[
            pltpu.VMEM((share, rows, 2 * width), BF16),
            pltpu.VMEM((width, keys_len), BF16),
            pltpu.VMEM((experts, width, hid), BF16),
            pltpu.VMEM((experts, strip, hidden), BF16),
            pltpu.VMEM((size, experts, strip, hid), BF16),
            pltpu.SemaphoreType.DMA((share,)),
            pltpu.SemaphoreType.DMA((share,)),
            pltpu.SemaphoreType.DMA,
            pltpu.SemaphoreType.DMA((size,)),
            pltpu.SemaphoreType.DMA((size,)),
        ]
        + entry_scratch,
        compiler_params=pltpu.CompilerParams(
            collective_id=5 + first, has_side_effects=True, vmem_limit_bytes=VMEM_LIMIT
        ),
        name="attention_forward_first" if first else "attention_forward",
    )(expert_in, *(entry or later))


def attention_backward(
    grad, back, back_tail, state, middle, message, gates, chosen, queries, kv, log_total, mixed,
    dense, length, up_grad, plan, job, last,
):
    rows, width = state.shape
    share = plan.share
    keys_len = rows * share
    heads = width // HEAD
    columns = dense.shape[1]
    swap = Swap(plan)
    strip = width // plan.dp
    dense_shape = (plan.dp // 2, 2, strip, columns)
    moves = up_grad is not None
    shift = Shift(up_grad) if moves else None
    moved_out = moves and not last

    def kernel(*refs):
        (
            grad_ref, back_ref, tail_ref, state_ref, mid_ref, msg_ref, gates_ref, chosen_ref, queries, kv,
            log_total, mixed, weights, length_ref,
        ), refs = refs[:14], refs[14:]
        if moves:
            up_ref, refs = refs[0], refs[1:]
        taken = len(job.args)
        job_refs, refs = refs[:taken], refs[taken:]
        (new_ref, new_low_ref, dense_ref), refs = refs[:3], refs[3:]
        if moved_out:
            moved_ref, refs = refs[0], refs[1:]
        job_outs, refs = refs[: len(job.out_shape)], refs[len(job.out_shape) :]
        (
            keys_t, normed_ref, grad_mid, grad_heads, grad_q, kv_grads, kv_got, grad_packed, send, recv,
        ), refs = refs[:10], refs[10:]
        if moves:
            moving = (up_ref, *refs[:3])
            refs = refs[3:]
        if last:
            (pieces, piece_sem), refs = refs[:2], refs[2:]
            if job.kinds:
                job_refs = (job_refs[0], moving[1], *job_refs[1:], dense_ref)
        summing = last and job.kinds
        job.bind(job_refs, job_outs, refs)
        in_heads, after_heads, after_sums, rest = job.share_out(HEAD_TICKS)
        me = lax.axis_index("dp")
        part = lax.rem(me, share)
        greet(
            *[({"dp": me ^ k}, None) for k in range(1, plan.dp if moves else share)],
            *job.peers(),
            *(swap.peers() if last else []),
        )
        if moves:
            shift.start(*moving)
        if job.kinds:
            job.begin("down")
        if summing:
            job.dense_begin(job.dense[0])
        rows_of = weight_rows(weights)
        gates = gates_ref[...]
        grad_gates = tail_ref[:, :rows] * chosen_ref[:, :rows]
        grad_logits = split_rows(gates * (grad_gates - row_sums(gates * grad_gates)))
        router = jnp.concatenate([rows_of[4:8], jnp.zeros((4, width), F32)], 0)
        twice = jnp.concatenate([router, router], 0).astype(BF16)
        grad_normed = back_ref[...] + dot(grad_logits, twice, TN)
        router_grad = dot(grad_logits, msg_ref[:rows])
        router_grad = router_grad[:8] + router_grad[8:]
        unit, inverse = normalize(mid_ref[...])
        gain_two = row_sums(grad_normed * unit)
        bias_two = row_sums(grad_normed)
        grad_mid[...] = grad_ref[...] + norm_back(grad_normed * rows_of[2:3], unit, inverse)
        low = grad_mid[...].astype(BF16)

        def put(columns_of, values):
            for at in range(plan.dp):
                dense_ref[at // 2, at % 2, :, columns_of] = values[at * strip : (at + 1) * strip].astype(BF16)

        put(slice(3 * width, 4 * width), dot(mixed[...], low))
        grad_heads[...] = dot(low, weights[:, 3 * width : 4 * width], NT).astype(BF16)
        for at in range(share):
            keys_t[:, at * rows : (at + 1) * rows] = jnp.transpose(kv[at, :, :width].astype(F32)).astype(BF16)
        key = lax.broadcasted_iota(jnp.int32, (keys_len, rows), 0)
        valid = key.astype(F32) < length_ref[0:1, 0:1]

        def pair_of_heads(pair, carry):
            lanes = pl.ds(pl.multiple_of(pair * 128, 128), 128)
            value_lanes = pl.ds(pl.multiple_of(width + pair * 128, 128), 128)
            keys_pair = kv[:, :, lanes].reshape(keys_len, 128)
            values_pair = kv[:, :, value_lanes].reshape(keys_len, 128)
            grad_k = jnp.zeros((keys_len, 128), F32)
            grad_v = jnp.zeros((keys_len, 128), F32)
            for parity in range(2):
                head = 2 * pair + parity
                query = one_head(queries[:, lanes], parity)
                pull = one_head(grad_heads[:, lanes], parity)
                scores = dot(keys_pair, query, NT)
                probs = jnp.where(valid, jnp.exp(scores - log_total[head]), 0.0)
                grad_probs = dot(values_pair, pull, NT)
                grad_scores = probs * (grad_probs - row_sums(probs * grad_probs))
                grad_scores = grad_scores.astype(BF16)
                grad_v += dot(probs.astype(BF16), pull)
                grad_k += dot(grad_scores, query)
                place = pl.ds(pl.multiple_of(head * HEAD, HEAD), HEAD)
                grad_q[place, :] = dot(keys_t[place, :], grad_scores) * HEAD ** (-0.5)
            kv_grads[:, :, lanes] = grad_k.astype(BF16).reshape(share, rows, 128)
            kv_grads[:, :, value_lanes] = grad_v.astype(BF16).reshape(share, rows, 128)
            for at, ticks in enumerate(in_heads):
                for tick in ticks:
                    pl.when(pair == at)(tick)
            if summing:
                pl.when(pair == heads // 2 - 2)(lambda: job.dense_near(job.dense[0]))
            return carry

        lax.fori_loop(0, heads // 2, pair_of_heads, 0)
        for tick in after_heads[0]:
            tick()
        copies = [
            remote(kv_grads.at[part ^ k], kv_got.at[k], send.at[k], recv.at[k], {"dp": me ^ k})
            for k in range(1, share)
        ]
        for copy in copies:
            copy.start()
        unit, inverse = normalize(state_ref[...])
        normed_ref[...] = (unit * rows_of[0:1] + rows_of[1:2]).astype(BF16)
        grad_packed[:, :width] = jnp.transpose(grad_q[...]).astype(BF16)
        for copy in copies:
            copy.wait()
        total = kv_grads[part].astype(F32)
        for k in range(1, share):
            total += kv_got[k].astype(F32)
        grad_packed[:, width:] = total.astype(BF16)
        grad_normed = dot(grad_packed[...], weights[:, : 3 * width], NT)
        for block in range(3):
            cols = slice(block * width, (block + 1) * width)
            put(cols, dot(normed_ref[...], grad_packed[:, cols], TN))
        gain_one = row_sums(grad_normed * unit)
        bias_one = row_sums(grad_normed)
        tail = jnp.concatenate([gain_one, bias_one, gain_two, bias_two, router_grad[:4]], 0)
        put(slice(4 * width, columns), pad_lanes(jnp.transpose(tail), columns - 4 * width))
        for tick in after_sums[0]:
            tick()
        if summing:
            job.dense_begin(job.dense[1])
            shift.arrive(*moving)
            job.begin("up")
        new = grad_mid[...] + norm_back(grad_normed * rows_of[0:1], unit, inverse)
        if last:
            for k in range(plan.images):
                new_low_ref[k] = new[k * plan.piece : (k + 1) * plan.piece].astype(BF16)
            swap.start(new_low_ref, pieces, piece_sem)
        else:
            new_low_ref[...] = new.astype(BF16)
            new_ref[...] = new
        if moved_out:
            shift.arrive(*moving)
            moved_ref[...] = moving[1][...]
        for at, tick in enumerate(rest, sum(map(sum, HEAD_TICKS))):
            if summing and at == DENSE_TICKS[0]:
                job.dense_near(job.dense[1])
            if summing and at == DENSE_TICKS[1]:
                job.dense_far(job.dense[0])
            if summing and at == DENSE_TICKS[2]:
                job.dense_far(job.dense[1])
            tick()
        job.finish()
        if moves:
            shift.drain(*moving)
        if last:
            swap.wait(new_low_ref, pieces, piece_sem)
            for k in range(plan.images):
                new_ref[k] = pieces[k].astype(F32)

    image_shape = (plan.images, plan.piece, width) if last else (rows, width)
    last_scratch = [
        pltpu.VMEM((plan.images, plan.piece, width), BF16),
        pltpu.SemaphoreType.DMA((2, plan.images)),
    ]
    return pl.pallas_call(
        kernel,
        out_shape=(
            jax.ShapeDtypeStruct(image_shape, F32),
            jax.ShapeDtypeStruct(image_shape, BF16),
            jax.ShapeDtypeStruct(dense_shape, BF16),
            *([jax.ShapeDtypeStruct(shift.shape, BF16)] if moved_out else []),
            *job.out_shape,
        ),
        in_specs=[in_vmem()] * (14 + moves + len(job.args)),
        out_specs=(in_vmem(),) * (3 + moved_out) + (in_any(),) * len(job.out_shape),
        scratch_shapes=[
            pltpu.VMEM((width, keys_len), BF16),
            pltpu.VMEM((rows, width), BF16),
            pltpu.VMEM((rows, width), F32),
            pltpu.VMEM((rows, width), BF16),
            pltpu.VMEM((width, rows), F32),
            pltpu.VMEM((share, rows, 2 * width), BF16),
            pltpu.VMEM((share, rows, 2 * width), BF16),
            pltpu.VMEM((rows, 3 * width), BF16),
            pltpu.SemaphoreType.DMA((share,)),
            pltpu.SemaphoreType.DMA((share,)),
        ]
        + (shift.scratch_shapes if moves else [])
        + (last_scratch if last else [])
        + job.scratch_shapes,
        compiler_params=pltpu.CompilerParams(
            collective_id=9 if last else 8, has_side_effects=True, vmem_limit_bytes=VMEM_LIMIT
        ),
        name="attention_backward_last" if last else "attention_backward",
    )(
        grad, back, back_tail, state, middle, message, gates, chosen, queries, kv, log_total, mixed,
        dense, length, *([up_grad] if moves else []), *job.args,
    )


def build(mesh):
    def shards(
        tokens,
        cotangent,
        routes,
        token_mask,
        ln1_gain,
        ln1_bias,
        qkv_weight,
        out_weight,
        ln2_gain,
        ln2_bias,
        router_weight,
        expert_in,
        expert_out,
    ):
        images, piece, width = tokens.shape
        levels, experts = expert_in.shape[:2]
        plan = Plan(mesh, images, token_mask.shape[1])
        rows = plan.rows
        wide = experts * expert_out.shape[2]
        lined = plan.seq == 4

        mine = lax.rem(lax.axis_index("seq"), images)
        chosen = jnp.sum((routes[..., None] == jnp.arange(experts, dtype=jnp.int32)).astype(F32), -2)
        chosen = jnp.transpose(chosen, (1, 0, 3, 2))
        at_slot = (jnp.arange(images) == mine).astype(F32)[:, None]
        chosen = (chosen[..., None, :] * at_slot).reshape(images, levels, experts, rows)
        chosen = jnp.pad(chosen, ((0, 0), (0, 0), (0, 8 - experts), (0, width - rows)))
        lengths = jnp.where(mine == 0, jnp.sum(token_mask, -1), 0)
        lengths = jnp.stack([lengths // 4, lengths % 4], -1).astype(F32)
        lengths = jnp.pad(lengths, ((0, 0), (0, 14)))[:, :, None]
        facts = jnp.concatenate(
            [chosen.reshape(images, 8 * levels, width), jnp.broadcast_to(lengths, (images, 16, width))], 1
        ).astype(BF16)

        vectors = jnp.stack([ln1_gain, ln1_bias, ln2_gain, ln2_bias], -1)
        tails = jnp.concatenate([vectors, router_weight], -1)
        tails = jnp.pad(tails, ((0, 0), (0, 0), (0, 128 - tails.shape[-1])))
        dense_own = jnp.concatenate([qkv_weight, out_weight, tails], -1)
        down_all = expert_out.reshape(levels, wide, width)

        saved = []
        for level in range(levels):
            if level:
                made = attention_forward(
                    plan, level, expert_in, later=(state, dense, chosen[level], length)
                )
            else:
                *made, grad, grad_low, state, chosen, length, dense = attention_forward(
                    plan, level, expert_in, entry=(tokens, facts, dense_own[level], cotangent)
                )
            message, middle, queries, kv, log_total, mixed, gates, up = made
            new_state, new_low, blocks, act, slope, *next_dense = experts_forward(
                message, middle, up, down_all[level], plan.dp,
                dense_own[level + 1] if level + 1 < levels else None,
            )
            attended = (
                state, middle, message, gates, chosen[level], queries, kv, log_total, mixed,
                dense, length,
            )
            dense = next_dense[0] if next_dense else None
            saved.append((attended, (blocks, act, slope, up, down_all[level])))
            state = new_state
        leaving = new_low.reshape(images, piece, width)

        sums = [None] * levels
        job = LineSums()
        for level in reversed(range(levels)):
            attended, routed = saved[level]
            last = level == 0
            back, back_tail, up_grad, down_grad, *others = experts_backward(
                grad_low, *routed, plan, job, leaving
            )
            if leaving is not None:
                output, *others = others
                leaving = None
            if job.kinds:
                downs, ups = jnp.concatenate([first_downs, others[0]]), others[1]
            up_grad = up_grad.reshape(experts, plan.dp, 4, width // plan.dp // 4, -1)
            down_grad = down_grad.reshape(16, wide // 16, width)
            job = LineSums(plan.dp, (0, 8), down=down_grad) if lined else LineSums()
            if lined and last:
                more = {} if level + 1 == levels else {"dense_more": dense_grad}
                job = LineSums(
                    plan.dp,
                    None,
                    down=down_grad,
                    up=jax.ShapeDtypeStruct(Shift(up_grad).shape, BF16),
                    **more,
                    dense=jax.ShapeDtypeStruct((plan.dp // 2, 2, width // plan.dp, dense_own.shape[-1]), BF16),
                )
            grad, grad_low, dense_grad, *others = attention_backward(
                grad, back, back_tail, *attended, up_grad if lined else None, plan, job, last
            )
            if not lined:
                sums[level] = sum_weights_plainly(plan.dp, down_grad, up_grad, dense_grad)
            elif last:
                sums[level] = (others[0], others[1], others[-1])
                sums[level + 1] = (downs, ups, others[2])
            else:
                first_downs = others[1]
                job = LineSums(plan.dp, (8, 16), down=down_grad, up=others[0])
        down_grad, up_grad, dense_grad = (
            jnp.stack([item.reshape(like.shape[1:]) for item in items]).astype(F32)
            for items, like in zip(zip(*sums), (expert_out, expert_in, dense_own))
        )
        return (
            output,
            grad,
            dense_grad[..., 4 * width],
            dense_grad[..., 4 * width + 1],
            dense_grad[..., : 3 * width],
            dense_grad[..., 3 * width : 4 * width],
            dense_grad[..., 4 * width + 2],
            dense_grad[..., 4 * width + 3],
            dense_grad[..., 4 * width + 4 : 4 * width + 4 + experts],
            up_grad,
            down_grad,
        )

    return shards


def solution(mesh):
    return jax.shard_map(
        build(mesh),
        mesh=mesh,
        in_specs=(
            P("dp", "seq", None),
            P("dp", "seq", None),
            P(None, "dp", "seq", None),
            P("dp", None),
            P(None, "dp"),
            P(None, "dp"),
            P(None, "dp", None),
            P(None, "dp", None),
            P(None, "dp"),
            P(None, "dp"),
            P(None, "dp", None),
            P(None, None, "dp", None),
            P(None, None, "dp", None),
        ),
        out_specs=(
            P("dp", "seq", None),
            P("dp", "seq", None),
            P(None, "dp"),
            P(None, "dp"),
            P(None, "dp", None),
            P(None, "dp", None),
            P(None, "dp"),
            P(None, "dp"),
            P(None, "dp", None),
            P(None, None, "dp", None),
            P(None, None, "dp", None),
        ),
        check_vma=False,
    )
```

profile of v0, /device:TPU:0, one launch (start us, length us, event | category | flops | bytes accessed | tf_op | source)
XLA Modules:
  0.0 394.6 jit_solution(4659824930688860244)
XLA Ops:
  0.6 0.0 copy-start
  0.7 1.0 reduce_sum.19
  1.6 0.1 copy.58
  1.7 0.1 add_convert_fusion
  1.8 0.1 mul.22
  1.9 0.1 mul.23
  2.0 0.7 convert_reduce_fusion
  2.7 0.1 mul.21
  2.9 0.1 broadcast_in_dim.17
  2.9 0.6 pad_maximum_fusion.1.refs_1_
  3.6 0.8 copy.62
  4.4 0.8 copy.63
  5.1 0.8 copy.64
  5.9 0.8 copy.65
  6.7 0.8 copy.66
  7.5 0.1 concatenate.14
  7.6 1.1 fusion.1
  8.7 0.8 slice_bitcast_fusion
  9.6 0.0 copy-done
  9.6 1.5 fusion.3
  11.1 35.1 %attention_forward_first.1 = (bf16[336,512]{1,0:T(8,128)(2,1)}, f32[320,512]{1,0:T(8,128)}, bf16[320,512]{1,0:T(8,128)(2,1)}, bf16[2,320,1024]{2,1,0:T(8,128)(2,...) custom-call(bf16[2,4,64,2048]{3,2,1,0:T(8,128)(2,1)} %in_ref.3, ...), custom_call_target="tpu_custom_call" | custom-call | tf_op jit(solution)/shard_map/attention_forward_first/pallas_call | solution.py:1028
  46.2 1.3 slice_bitcast_fusion.2
  47.5 45.8 %experts_forward.2 = (f32[320,512]{1,0:T(8,128)}, bf16[320,512]{1,0:T(8,128)(2,1)}, bf16[8,336,512]{2,1,0:T(8,128)(2,1)}, bf16[8,320,1024]{2,1,0:T(8,128)(2,1)},...) custom-call(bf16[336,512]{1,0:T(8,128)(2,1)} %get-tuple-element.64.msg_ref.refs_5_, ...), custom_call_target="tpu_custom_call" | custom-call | tf_op jit(solution)/shard_map/experts_forward/pallas_call | solution.py:443
  93.3 19.0 %attention_forward.1 = (bf16[336,512]{1,0:T(8,128)(2,1)}, f32[320,512]{1,0:T(8,128)}, bf16[320,512]{1,0:T(8,128)(2,1)}, bf16[2,320,1024]{2,1,0:T(8,128)(2,1)}, f...) custom-call(bf16[2,4,64,2048]{3,2,1,0:T(8,128)(2,1)} %in_ref.3, ...), custom_call_target="tpu_custom_call" | custom-call | tf_op jit(solution)/shard_map/attention_forward/pallas_call | solution.py:1028
  112.3 40.5 %experts_forward.3 = (f32[320,512]{1,0:T(8,128)}, bf16[320,512]{1,0:T(8,128)(2,1)}, bf16[8,336,512]{2,1,0:T(8,128)(2,1)}, bf16[8,320,1024]{2,1,0:T(8,128)(2,1)}, bf16[8,320,1024]{2,1,0:T(8,128)(2,1)}) custom-call(bf16[336,512]{1,0:T(8,128)(2,1)} %get-tuple-element.71.msg_ref.refs_5_, f32[320,512]{1,0:T(8,128)} %get-tuple-element.72.mid_ref.refs_4_, ...), custom_call_target="tpu_custom_call" | custom-call | tf_op jit(solution)/shard_map/experts_forward/pallas_call | solution.py:443
  152.8 39.8 %experts_backward.1 = (f32[320,512]{1,0:T(8,128)}, f32[8,512]{1,0:T(8,128)}, bf16[4,512,256]{2,1,0:T(8,128)(2,1)}, bf16[1024,512]{1,0:T(8,128)(2,1)}, bf16[2,160,512]{2,1,0:T(8,128)(2,1)}) custom-call(bf16[320,512]{1,0:T(8,128)(2,1)} %get-tuple-element.63.refs_0_, bf16[8,336,512]{2,1,0:T(8,128)(2,1)} %get-tuple-element.74.refs_1_, ...), custom_call_target="tpu_custom_call" | custom-call | tf_op jit(solution)/shard_map/experts_backward/pallas_call | solution.py:832
  192.6 33.9 %attention_backward.1 = (f32[320,512]{1,0:T(8,128)}, bf16[320,512]{1,0:T(8,128)(2,1)}, bf16[4,2,64,2176]{3,2,1,0:T(8,128)(2,1)}, bf16[4,4,16,2048]{3,2,1,0:T(8,128)(2,1)}, bf16[8,64,512]{2,1,0:T(8,128)(2,1)}) custom-call(f32[320,512]{1,0:T(8,128)} %get-tuple-element.79.refs_0_, f32[320,512]{1,0:T(8,128)} %get-tuple-element.80.refs_1_, ...), custom_call_target="tpu_custom_call" | custom-call | tf_op jit(solution)/shard_map/attention_backward/pallas_call | solution.py:1237
  226.5 64.1 %experts_backward_and_sums.1 = (f32[320,512]{1,0:T(8,128)}, f32[8,512]{1,0:T(8,128)}, bf16[4,512,256]{2,1,0:T(8,128)(2,1)}, bf16[1024,512]{1,0:T(8,128)(2,1)}, b...) custom-call(bf16[320,512]{1,0:T(8,128)(2,1)} %get-tuple-element.90.refs_0_, ...), custom_call_target="tpu_custom_call" | custom-call | tf_op jit(solution)/shard_map/experts_backward_and_sums/pallas_call | solution.py:832
  290.6 0.0 copy-start.4
  290.6 0.0 copy-start.5
  290.6 90.8 %attention_backward_last.1 = (f32[2,160,512]{2,1,0:T(8,128)}, bf16[2,160,512]{2,1,0:T(8,128)(2,1)}, bf16[4,2,64,2176]{3,2,1,0:T(8,128)(2,1)}, bf16[16,64,512]{2,...) custom-call(f32[320,512]{1,0:T(8,128)} %get-tuple-element.89.refs_0_, ...), custom_call_target="tpu_custom_call" | custom-call | tf_op jit(solution)/shard_map/attention_backward_last/pallas_call | solution.py:1237
  381.4 0.0 copy-start.7
  381.4 1.3 copy.67
  382.8 0.0 copy-done.4
  382.8 0.0 copy-done.5
  382.8 0.1 pad_maximum_fusion
  382.9 0.0 copy-done.7
  382.9 0.3 copy.68
  383.2 0.6 maximum_convert_fusion.3
  383.8 0.6 maximum_convert_fusion.4
  384.4 0.3 maximum_convert_fusion.2
  384.8 0.1 slice.59
  384.9 1.3 copy.69
  386.2 0.9 copy.70
  387.1 3.7 maximum_convert_fusion.1
  390.8 2.3 maximum_convert_fusion
  393.1 0.7 copy.73
  393.8 0.8 copy.74
  (17 shorter events, 0.1 us)
Async XLA Ops:
  0.6 8.9 %copy-start = (bf16[2,4,256,512]{3,2,1,0:T(8,128)(2,1)S(1)}, bf16[2,4,256,512]{3,2,1,0:T(8,128)(2,1)}, u32[]{:S(2)}) copy-start(bf16[2,4,256,512]{3,2,1,0:T(8,128)(2,1)} %param.25) | copy-start | bytes 6291460
  290.6 92.2 %copy-start.4 = (bf16[8,64,512]{2,1,0:T(8,128)(2,1)S(1)}, bf16[8,64,512]{2,1,0:T(8,128)(2,1)}, u32[]{:S(2)}) copy-start(bf16[8,64,512]{2,1,0:T(8,128)(2,1)} %get-tuple-element.113) | copy-start | bytes 1572868
  290.6 92.1 %copy-start.5 = (bf16[8,64,512]{2,1,0:T(8,128)(2,1)S(1)}, bf16[8,64,512]{2,1,0:T(8,128)(2,1)}, u32[]{:S(2)}) copy-start(bf16[8,64,512]{2,1,0:T(8,128)(2,1)} %get-tuple-element.114) | copy-start | bytes 1572868
  381.4 1.4 copy-start.7
  387.1 3.7 copy-start.1
  387.1 3.7 copy-start.2
  390.8 2.3 copy-start.6
  390.8 3.0 copy-start.3
where the time goes:
time: 395 us
  Pallas kernels  369 us (93%)
  local copies, waits for them, and re-layouts  13.8 us (3%)
  other arithmetic  11.1 us (3%)
    pallas_call x2, Pallas kernels, attention_backward(): pl.pallas_call(kernel, out_shape=(jax.ShapeDtypeStruct(image_shape, F32),...  125 us
    pallas_call x2, Pallas kernels, experts_backward(): pl.pallas_call(kernel, out_shape=(jax.ShapeDtypeStruct((rows, width), F32...  104 us
    pallas_call x2, Pallas kernels, experts_forward(): pl.pallas_call(kernel, out_shape=(jax.ShapeDtypeStruct((rows, width), F32...  86.3 us
    pallas_call x2, Pallas kernels, attention_forward(): pl.pallas_call(kernel, out_shape=(jax.ShapeDtypeStruct((rows + 16, width)...  54 us

commit v1 on v0

--- a/solution.py
+++ b/solution.py
@@ -17,6 +17,7 @@
 EXPERT_TICKS = ((0, 2, 1, 1, 1, 1, 1, 1), (1, 0, 1, 0), (1,), (1, 1, 0))
 HEAD_TICKS = ((0, 1, 1, 1), (1,), (1,))
 DENSE_TICKS = (5, 6, 14)
+EARLY_CHUNKS = 4
 NT = ((1,), (1,))
 TN = ((0,), (0,))
 
@@ -109,6 +110,18 @@
 def weight_rows(dense_ref):
     width = dense_ref.shape[0]
     return jnp.transpose(dense_ref[:, 4 * width :].astype(F32))
+
+
+def lay_strip(refs, level, dense, place):
+    packed, out, router, *vectors = refs
+    strip, width = out.shape[1:]
+    dense[place, : 3 * width] = packed[level]
+    dense[place, 3 * width : 4 * width] = out[level]
+    rows = [vector[...].astype(F32)[level : level + 1] for vector in vectors]
+    rows = jnp.concatenate(rows + [jnp.zeros((4, strip), F32)], 0)
+    columns = jnp.transpose(pad_lanes(rows, 128))[:strip, :4]
+    tail = jnp.concatenate([columns, router[level].astype(F32)], 1)
+    dense[place, 4 * width :] = pad_lanes(tail, 128).astype(BF16)
 
 
 class Plan:
@@ -329,37 +342,41 @@
         def step(at, carry):
             turn = at // 2
             pair = self.pair_at(turn)
-            even = lax.rem(at, 2) == 0
-            slot = 2 * pair + lax.rem(at, 2)
-
-            @pl.when(even & (turn > 0))
+            odd = lax.rem(at, 2) == 0
+            slot = 2 * pair + 1 - lax.rem(at, 2)
+
+            @pl.when(odd & (turn == 1))
+            def _():
+                for bit in self.bits:
+                    self.arrive(bit)
+
+            @pl.when(odd & (turn > len(self.bits)))
             def _():
                 self.arrive(pair)
-                settle(self.pair_at(turn - 1))
-
-            @pl.when(jnp.logical_not(even))
+
+            @pl.when(odd)
             def _():
                 self.handed(pair).wait_recv()
 
             total, total_tail = compute(slot, at)
 
-            @pl.when(even)
-            def _():
-                self.own[pair] = total
-                if tail:
-                    self.own_tail[pair] = total_tail
-
-            @pl.when(jnp.logical_not(even))
+            @pl.when(odd)
             def _():
                 self.give[pair, :rows] = total.astype(BF16)
                 if tail:
                     self.give[pair, rows:] = split_rows(total_tail)
                 self.given(pair).start()
 
+            @pl.when(jnp.logical_not(odd))
+            def _():
+                self.own[pair] = total
+                if tail:
+                    self.own_tail[pair] = total_tail
+                settle(pair)
+
             return carry
 
         lax.fori_loop(0, self.size, step, 0)
-        settle(self.order[-1])
 
     def collect(self, between=()):
         rows, tail = self.sizes
@@ -377,27 +394,32 @@
         self.drain()
 
 
-def experts_forward(message, middle, up, down, size, strip=None):
+def experts_forward(message, middle, up, down, level, size, strips=()):
     rows, width = middle.shape
     experts, _, hid = up.shape
     wide = experts * hid
     group = Group(size)
     spread = Spread(size)
-    extra = [] if strip is None else [strip]
-
-    def kernel(msg_ref, mid_ref, up_ref, down_ref, *refs):
-        strip_ref, refs = refs[: len(extra)], refs[len(extra) :]
+    extra = bool(strips)
+    strip = width // size
+
+    def kernel(msg_ref, mid_ref, up_ref, down_all, *refs):
+        strip_refs, refs = refs[: len(strips)], refs[len(strips) :]
         (out_ref, low_ref, all_ref, act_ref, slope_ref), refs = refs[:5], refs[5:]
-        dense_ref, refs = refs[: len(extra)], refs[len(extra) :]
-        (slots, act, slope, scaled, save_sem), refs = refs[:5], refs[5:]
+        if extra:
+            dense_ref, refs = refs[0], refs[1:]
+        (down_ref, down_sem, slots, act, slope, scaled, save_sem), refs = refs[:7], refs[7:]
         scratch, refs = refs[:13], refs[13:]
+        bring = pltpu.make_async_copy(down_all.at[level], down_ref, down_sem)
+        bring.start()
         if extra:
             dense_all, keep_sem, *sems = refs
             me = lax.axis_index("dp")
-            spread.bind(Strips(dense_all, strip.shape[0]), sems)
-            dense_all[pl.ds(pl.multiple_of(me * strip.shape[0], 16), strip.shape[0])] = strip_ref[0][...]
+            spread.bind(Strips(dense_all, strip), sems)
+            lay_strip(strip_refs, level + 1, dense_all, pl.ds(pl.multiple_of(me * strip, 16), strip))
         greet(*group.peers())
         slots[0] = msg_ref[...]
+        bring.wait()
 
         def saves(slot):
             return (
@@ -427,7 +449,7 @@
         if extra:
             for pair in spread.order:
                 spread.handed(pair).wait_recv()
-            keep = pltpu.make_async_copy(dense_all, dense_ref[0], keep_sem)
+            keep = pltpu.make_async_copy(dense_all, dense_ref, keep_sem)
             keep.start()
         group.collect()
         out = mid_ref[...] + group.own[0]
@@ -448,11 +470,13 @@
             jax.ShapeDtypeStruct((size, rows + 16, width), BF16),
             jax.ShapeDtypeStruct((size, rows, wide), BF16),
             jax.ShapeDtypeStruct((size, rows, wide), BF16),
-            *[jax.ShapeDtypeStruct((size * item.shape[0], item.shape[1]), BF16) for item in extra],
+            *([jax.ShapeDtypeStruct((width, 4 * width + 128), BF16)] if extra else []),
         ),
-        in_specs=[in_vmem()] * (4 + len(extra)),
-        out_specs=(in_vmem(), in_vmem(), in_any(), in_any(), in_any()) + (in_any(),) * len(extra),
+        in_specs=[in_vmem()] * 3 + [in_any()] + [in_vmem()] * len(strips),
+        out_specs=(in_vmem(), in_vmem(), in_any(), in_any(), in_any()) + (in_any(),) * extra,
         scratch_shapes=[
+            pltpu.VMEM((wide, width), BF16),
+            pltpu.SemaphoreType.DMA,
             pltpu.VMEM((size, rows + 16, width), BF16),
             pltpu.VMEM((size, rows, wide), BF16),
             pltpu.VMEM((size, rows, wide), BF16),
@@ -461,7 +485,7 @@
         ]
         + group.scratch(rows, 0, width)
         + (
-            [pltpu.VMEM((size * strip.shape[0], strip.shape[1]), BF16), pltpu.SemaphoreType.DMA]
+            [pltpu.VMEM((width, 4 * width + 128), BF16), pltpu.SemaphoreType.DMA]
             + spread.semaphores()
             if extra
             else []
@@ -470,7 +494,7 @@
             collective_id=10 if extra else 1, has_side_effects=True, vmem_limit_bytes=VMEM_LIMIT
         ),
         name="experts_forward",
-    )(message, middle, up, down, *extra)
+    )(message, middle, up, down, *strips)
 
 
 class Shift:
@@ -506,8 +530,9 @@
 
 
 class LineSums:
-    def __init__(self, dp=0, down_chunks=None, **arrays):
+    def __init__(self, dp=0, down_chunks=None, kept=(), **arrays):
         self.dp = dp
+        self.kept = kept
         self.first = down_chunks[0] if down_chunks else 0
         self.kinds = list(arrays)
         self.args = tuple(array for array in arrays.values() if not isinstance(array, jax.ShapeDtypeStruct))
@@ -533,7 +558,8 @@
                     pltpu.SemaphoreType.DMA((2, dp // 2)),
                 ]
             count, chunk = self.count[kind], self.chunk[kind]
-            self.out_shape += (jax.ShapeDtypeStruct((count,) + chunk, BF16),)
+            if kind not in kept:
+                self.out_shape += (jax.ShapeDtypeStruct((count,) + chunk, BF16),)
             self.scratch_shapes += [
                 pltpu.VMEM((count,) + chunk, BF16),
                 pltpu.VMEM((count // 2,) + chunk, BF16),
@@ -559,7 +585,7 @@
 
     def bind(self, refs, outs, scratch):
         self.refs = dict(zip(self.kinds, refs))
-        self.outs = dict(zip(self.kinds, outs))
+        self.outs = dict(zip((kind for kind in self.kinds if kind not in self.kept), outs))
         self.boxes = {}
         for kind in self.kinds:
             held = 14 if kind in self.dense else 9
@@ -695,7 +721,7 @@
                     self.inward(kind, c).wait_send()
 
         copies = [
-            pltpu.make_async_copy(self.boxes[kind][3], self.outs[kind], self.boxes[kind][8]) for kind in self.kinds
+            pltpu.make_async_copy(self.boxes[kind][3], out, self.boxes[kind][8]) for kind, out in self.outs.items()
         ]
         for copy in copies:
             copy.start()
@@ -724,7 +750,7 @@
     return lax.psum(down, "seq"), lax.psum(up.reshape(experts, quarters * r, -1), "seq"), lax.psum(dense, "seq")
 
 
-def experts_backward(grad, blocks, act, slope, up, down, plan, job, leaving=None):
+def experts_backward(grad, blocks, act, slope, up, down, level, plan, job, leaving=None):
     rows, width = grad.shape
     experts, _, hid = up.shape
     wide = experts * hid
@@ -734,7 +760,7 @@
     extra = [] if leaving is None else [leaving]
 
     def kernel(*refs):
-        (grad_ref, blocks_ref, act_ref, slope_ref, up_ref, down_ref), refs = refs[:6], refs[6:]
+        (grad_ref, blocks_ref, act_ref, slope_ref, up_ref, down_all), refs = refs[:6], refs[6:]
         if extra:
             leaving_ref, refs = refs[0], refs[1:]
         job_refs, refs = refs[: len(job.args)], refs[len(job.args) :]
@@ -742,8 +768,10 @@
         if extra:
             left_ref, refs = refs[0], refs[1:]
         job_outs, refs = refs[: len(job.args)], refs[len(job.args) :]
-        slots, blocks, facts, act, slope, weighed, scaled, pre, flat, load_sem = refs[:10]
-        refs = refs[10:]
+        slots, blocks, facts, act, slope, weighed, scaled, pre, flat, load_sem, down_ref, down_sem = refs[:12]
+        refs = refs[12:]
+        bring = pltpu.make_async_copy(down_all.at[level], down_ref, down_sem)
+        bring.start()
         scratch, refs = refs[:13], refs[13:]
         if extra:
             (left, left_sem), refs = refs[:2], refs[2:]
@@ -752,7 +780,7 @@
 
         def loads(at):
             two = lax.rem(at, 2)
-            slot = 2 * group.pair_at(at // 2) + two
+            slot = 2 * group.pair_at(at // 2) + 1 - two
             place = pl.ds(pl.multiple_of(slot * rows, 16), rows)
             return (
                 pltpu.make_async_copy(blocks_ref.at[slot, pl.ds(0, rows)], blocks.at[place], load_sem.at[two, 0]),
@@ -769,6 +797,7 @@
             swap.start(leaving_ref, left, left_sem)
         for expert in range(experts):
             flat[:, expert * hid : (expert + 1) * hid] = up_ref[expert]
+        bring.wait()
         lane = lax.broadcasted_iota(jnp.int32, (16, wide), 1) // hid
         pick = (lane == lax.broadcasted_iota(jnp.int32, (16, wide), 0)).astype(F32).astype(BF16)
 
@@ -839,7 +868,7 @@
             *left_shape,
             *job.out_shape,
         ),
-        in_specs=[in_vmem(), in_any(), in_any(), in_any(), in_vmem(), in_vmem()]
+        in_specs=[in_vmem(), in_any(), in_any(), in_any(), in_vmem(), in_any()]
         + [in_vmem()] * (len(extra) + len(job.args)),
         out_specs=(in_vmem(),) * (4 + len(extra)) + (in_any(),) * len(job.args),
         scratch_shapes=[
@@ -853,6 +882,8 @@
             pltpu.VMEM((size * rows, wide), BF16),
             pltpu.VMEM((width, wide), BF16),
             pltpu.SemaphoreType.DMA((2, 4)),
+            pltpu.VMEM((wide, width), BF16),
+            pltpu.SemaphoreType.DMA,
         ]
         + group.scratch(rows, 16, width)
         + (left_scratch if extra else [])
@@ -871,13 +902,15 @@
     levels, experts, strip, hidden = expert_in.shape
     spread = Spread(size)
     width = strip * size
-    columns = (entry or later)[1 + first].shape[-1]
+    columns = 4 * width + 128
     keys_len = rows * share
     heads = width // HEAD
     hid = hidden // size
 
+    given = entry or later
+
     def kernel(in_ref, *refs):
-        taken, refs = refs[:4], refs[4:]
+        taken, refs = refs[: len(given)], refs[len(given) :]
         (message, middle, queries, kv, log_total, mixed, gates_ref, up_ref), refs = refs[:8], refs[8:]
         if first:
             (grad, grad_low, state_ref, chosen_all, length_ref, dense_out), refs = refs[:6], refs[6:]
@@ -895,9 +928,9 @@
             )
 
         if first:
-            tokens_ref, facts_ref, dense_ref, cot_ref = taken
+            tokens_ref, facts_ref, cot_ref, *strips = taken
             tok, fact, cot, dense_all, tok_sem, fact_sem, cot_sem, keep_sem, *sems = refs
-            dense_all[pl.ds(pl.multiple_of(me * strip, 16), strip)] = dense_ref[...]
+            lay_strip(strips, level, dense_all, pl.ds(pl.multiple_of(me * strip, 16), strip))
             spread.bind(Strips(dense_all, strip), sems)
             spread.start()
             swap.start(facts_ref, fact, fact_sem)
@@ -1038,7 +1071,7 @@
             jax.ShapeDtypeStruct((experts, width, hid), BF16),
             *entry_out,
         ),
-        in_specs=[in_any()] + [in_vmem()] * 4,
+        in_specs=[in_any()] + [in_vmem()] * len(given),
         out_specs=(in_vmem(),) * 3 + (in_any(),) + (in_vmem(),) * 3 + (in_any(),) + entry_specs,
         scratch_shapes=[
             pltpu.VMEM((share, rows, 2 * width), BF16),
@@ -1057,7 +1090,7 @@
             collective_id=5 + first, has_side_effects=True, vmem_limit_bytes=VMEM_LIMIT
         ),
         name="attention_forward_first" if first else "attention_forward",
-    )(expert_in, *(entry or later))
+    )(expert_in, *given)
 
 
 def attention_backward(
@@ -1075,6 +1108,10 @@
     moves = up_grad is not None
     shift = Shift(up_grad) if moves else None
     moved_out = moves and not last
+    totals_shape = [
+        jax.ShapeDtypeStruct((len(job.kept), strip, wide), F32)
+        for wide in ((3 * width, width, columns - 4 * width) if job.kept else ())
+    ]
 
     def kernel(*refs):
         (
@@ -1088,6 +1125,8 @@
         (new_ref, new_low_ref, dense_ref), refs = refs[:3], refs[3:]
         if moved_out:
             moved_ref, refs = refs[0], refs[1:]
+        if totals_shape:
+            totals, refs = refs[:3], refs[3:]
         job_outs, refs = refs[: len(job.out_shape)], refs[len(job.out_shape) :]
         (
             keys_t, normed_ref, grad_mid, grad_heads, grad_q, kv_grads, kv_got, grad_packed, send, recv,
@@ -1222,6 +1261,14 @@
                 job.dense_far(job.dense[1])
             tick()
         job.finish()
+        for at, kind in enumerate(job.kept):
+            start = 0
+            for total in totals:
+                wide = total.shape[2]
+                for chunk in range(4):
+                    place = slice(chunk * strip // 4, (chunk + 1) * strip // 4)
+                    total[at, place] = job.boxes[kind][3][chunk, :, start : start + wide].astype(F32)
+                start += wide
         if moves:
             shift.drain(*moving)
         if last:
@@ -1241,10 +1288,11 @@
             jax.ShapeDtypeStruct(image_shape, BF16),
             jax.ShapeDtypeStruct(dense_shape, BF16),
             *([jax.ShapeDtypeStruct(shift.shape, BF16)] if moved_out else []),
+            *totals_shape,
             *job.out_shape,
         ),
         in_specs=[in_vmem()] * (14 + moves + len(job.args)),
-        out_specs=(in_vmem(),) * (3 + moved_out) + (in_any(),) * len(job.out_shape),
+        out_specs=(in_vmem(),) * (3 + moved_out + len(totals_shape)) + (in_any(),) * len(job.out_shape),
         scratch_shapes=[
             pltpu.VMEM((width, keys_len), BF16),
             pltpu.VMEM((rows, width), BF16),
@@ -1306,10 +1354,7 @@
             [chosen.reshape(images, 8 * levels, width), jnp.broadcast_to(lengths, (images, 16, width))], 1
         ).astype(BF16)
 
-        vectors = jnp.stack([ln1_gain, ln1_bias, ln2_gain, ln2_bias], -1)
-        tails = jnp.concatenate([vectors, router_weight], -1)
-        tails = jnp.pad(tails, ((0, 0), (0, 0), (0, 128 - tails.shape[-1])))
-        dense_own = jnp.concatenate([qkv_weight, out_weight, tails], -1)
+        strips = (qkv_weight, out_weight, router_weight, ln1_gain, ln1_bias, ln2_gain, ln2_bias)
         down_all = expert_out.reshape(levels, wide, width)
 
         saved = []
@@ -1320,19 +1365,18 @@
                 )
             else:
                 *made, grad, grad_low, state, chosen, length, dense = attention_forward(
-                    plan, level, expert_in, entry=(tokens, facts, dense_own[level], cotangent)
+                    plan, level, expert_in, entry=(tokens, facts, cotangent, *strips)
                 )
             message, middle, queries, kv, log_total, mixed, gates, up = made
             new_state, new_low, blocks, act, slope, *next_dense = experts_forward(
-                message, middle, up, down_all[level], plan.dp,
-                dense_own[level + 1] if level + 1 < levels else None,
+                message, middle, up, down_all, level, plan.dp, strips if level + 1 < levels else ()
             )
             attended = (
                 state, middle, message, gates, chosen[level], queries, kv, log_total, mixed,
                 dense, length,
             )
             dense = next_dense[0] if next_dense else None
-            saved.append((attended, (blocks, act, slope, up, down_all[level])))
+            saved.append((attended, (blocks, act, slope, up, down_all)))
             state = new_state
         leaving = new_low.reshape(images, piece, width)
 
@@ -1342,7 +1386,7 @@
             attended, routed = saved[level]
             last = level == 0
             back, back_tail, up_grad, down_grad, *others = experts_backward(
-                grad_low, *routed, plan, job, leaving
+                grad_low, *routed, level, plan, job, leaving
             )
             if leaving is not None:
                 output, *others = others
@@ -1351,16 +1395,16 @@
                 downs, ups = jnp.concatenate([first_downs, others[0]]), others[1]
             up_grad = up_grad.reshape(experts, plan.dp, 4, width // plan.dp // 4, -1)
             down_grad = down_grad.reshape(16, wide // 16, width)
-            job = LineSums(plan.dp, (0, 8), down=down_grad) if lined else LineSums()
+            job = LineSums(plan.dp, (0, EARLY_CHUNKS), down=down_grad) if lined else LineSums()
             if lined and last:
-                more = {} if level + 1 == levels else {"dense_more": dense_grad}
                 job = LineSums(
                     plan.dp,
                     None,
+                    ("dense", "dense_more"),
                     down=down_grad,
                     up=jax.ShapeDtypeStruct(Shift(up_grad).shape, BF16),
-                    **more,
-                    dense=jax.ShapeDtypeStruct((plan.dp // 2, 2, width // plan.dp, dense_own.shape[-1]), BF16),
+                    dense_more=dense_grad,
+                    dense=jax.ShapeDtypeStruct(dense_grad.shape, BF16),
                 )
             grad, grad_low, dense_grad, *others = attention_backward(
                 grad, back, back_tail, *attended, up_grad if lined else None, plan, job, last
@@ -1368,25 +1412,30 @@
             if not lined:
                 sums[level] = sum_weights_plainly(plan.dp, down_grad, up_grad, dense_grad)
             elif last:
-                sums[level] = (others[0], others[1], others[-1])
-                sums[level + 1] = (downs, ups, others[2])
+                packed_grad, out_grad, tail_grad = others[:3]
+                sums[level] = others[3:]
+                sums[level + 1] = (downs, ups)
             else:
                 first_downs = others[1]
-                job = LineSums(plan.dp, (8, 16), down=down_grad, up=others[0])
-        down_grad, up_grad, dense_grad = (
+                job = LineSums(plan.dp, (EARLY_CHUNKS, 16), down=down_grad, up=others[0])
+        down_grad, up_grad = (
             jnp.stack([item.reshape(like.shape[1:]) for item in items]).astype(F32)
-            for items, like in zip(zip(*sums), (expert_out, expert_in, dense_own))
+            for items, like in zip(zip(*(item[:2] for item in sums)), (expert_out, expert_in))
         )
+        if not lined:
+            dense_grad = jnp.stack([item[2].reshape(width // plan.dp, -1) for item in sums]).astype(F32)
+            packed_grad, out_grad = dense_grad[..., : 3 * width], dense_grad[..., 3 * width : 4 * width]
+            tail_grad = dense_grad[..., 4 * width :]
         return (
             output,
             grad,
-            dense_grad[..., 4 * width],
-            dense_grad[..., 4 * width + 1],
-            dense_grad[..., : 3 * width],
-            dense_grad[..., 3 * width : 4 * width],
-            dense_grad[..., 4 * width + 2],
-            dense_grad[..., 4 * width + 3],
-            dense_grad[..., 4 * width + 4 : 4 * width + 4 + experts],
+            tail_grad[..., 0],
+            tail_grad[..., 1],
+            packed_grad,
+            out_grad,
+            tail_grad[..., 2],
+            tail_grad[..., 3],
+            tail_grad[..., 4 : 4 + experts],
             up_grad,
             down_grad,
         )

time: 395 us -> 381 us (0.965)
  Pallas kernels: 369 us -> 362 us
  other arithmetic: 11.1 us -> 6.95 us
    pallas_call x2, Pallas kernels: 125 us -> 118 us  [attention_backward(): pl.pallas_call(kernel, out_shape=(jax.ShapeDtypeStruct(image_shape, F32),...]
    another operation x7 -> x1, local copies, waits for them, and re-layouts: 4.72 us -> 0.01 us  [the longest x4 3.08 us: shards(): vectors = jnp.stack([ln1_gain, ln1_bias, ln2_gain, ln2_bias], -1)]
where the time goes in v1:
time: 381 us; the launch traced here: 380 us
  Pallas kernels  362 us (95%)
  local copies, waits for them, and re-layouts  9.92 us (3%)
  other arithmetic  6.95 us (2%)
    pallas_call x2, Pallas kernels, attention_backward(): pl.pallas_call(kernel, out_shape=(jax.ShapeDtypeStruct(image_shape, F32),...  118 us
    pallas_call x2, Pallas kernels, experts_backward(): pl.pallas_call(kernel, out_shape=(jax.ShapeDtypeStruct((rows, width), F32...  107 us
    pallas_call x2, Pallas kernels, experts_forward(): pl.pallas_call(kernel, out_shape=(jax.ShapeDtypeStruct((rows, width), F32...  82.8 us
    pallas_call x2, Pallas kernels, attention_forward(): pl.pallas_call(kernel, out_shape=(jax.ShapeDtypeStruct((rows + 16, width)...  54.2 us

profile of v1, /device:TPU:0, one launch (start us, length us, event | category | flops | bytes accessed | tf_op | source)
XLA Modules:
  0.0 379.9 jit_solution(12910869058100969102)
XLA Ops:
  0.7 0.8 reduce_sum.19
  1.5 0.1 copy.40
  1.6 0.1 add_convert_fusion
  1.7 0.1 mul.22
  1.8 0.1 mul.23
  1.8 0.7 convert_reduce_fusion
  2.6 0.1 mul.21
  2.7 0.1 broadcast_in_dim.17
  2.8 0.6 pad_maximum_fusion.1.refs_1_
  3.4 1.4 copy.44.refs_5_.refs_2_
  4.8 35.3 %attention_forward_first.1 = (bf16[336,512]{1,0:T(8,128)(2,1)}, f32[320,512]{1,0:T(8,128)}, bf16[320,512]{1,0:T(8,128)(2,1)}, bf16[2,320,1024]{2,1,0:T(8,128)(2,...) custom-call(bf16[2,4,64,2048]{3,2,1,0:T(8,128)(2,1)} %in_ref.3, ...), custom_call_target="tpu_custom_call" | custom-call | tf_op jit(solution)/shard_map/attention_forward_first/pallas_call | solution.py:1061
  40.1 1.3 slice_bitcast_fusion
  41.4 43.6 %experts_forward.2 = (f32[320,512]{1,0:T(8,128)}, bf16[320,512]{1,0:T(8,128)(2,1)}, bf16[8,336,512]{2,1,0:T(8,128)(2,1)}, bf16[8,320,1024]{2,1,0:T(8,128)(2,1)},...) custom-call(bf16[336,512]{1,0:T(8,128)(2,1)} %get-tuple-element.65.msg_ref.refs_5_, ...), custom_call_target="tpu_custom_call" | custom-call | tf_op jit(solution)/shard_map/experts_forward/pallas_call | solution.py:465
  85.0 19.0 %attention_forward.1 = (bf16[336,512]{1,0:T(8,128)(2,1)}, f32[320,512]{1,0:T(8,128)}, bf16[320,512]{1,0:T(8,128)(2,1)}, bf16[2,320,1024]{2,1,0:T(8,128)(2,1)}, f...) custom-call(bf16[2,4,64,2048]{3,2,1,0:T(8,128)(2,1)} %in_ref.3, ...), custom_call_target="tpu_custom_call" | custom-call | tf_op jit(solution)/shard_map/attention_forward/pallas_call | solution.py:1061
  104.0 39.2 %experts_forward.3 = (f32[320,512]{1,0:T(8,128)}, bf16[320,512]{1,0:T(8,128)(2,1)}, bf16[8,336,512]{2,1,0:T(8,128)(2,1)}, bf16[8,320,1024]{2,1,0:T(8,128)(2,1)}, bf16[8,320,1024]{2,1,0:T(8,128)(2,1)}) custom-call(bf16[336,512]{1,0:T(8,128)(2,1)} %get-tuple-element.72.msg_ref.refs_5_, f32[320,512]{1,0:T(8,128)} %get-tuple-element.73.mid_ref.refs_4_, ...), custom_call_target="tpu_custom_call" | custom-call | tf_op jit(solution)/shard_map/experts_forward/pallas_call | solution.py:465
  143.3 39.1 %experts_backward.1 = (f32[320,512]{1,0:T(8,128)}, f32[8,512]{1,0:T(8,128)}, bf16[4,512,256]{2,1,0:T(8,128)(2,1)}, bf16[1024,512]{1,0:T(8,128)(2,1)}, bf16[2,160,512]{2,1,0:T(8,128)(2,1)}) custom-call(bf16[320,512]{1,0:T(8,128)(2,1)} %get-tuple-element.64.refs_0_, bf16[8,336,512]{2,1,0:T(8,128)(2,1)} %get-tuple-element.75.refs_1_, ...), custom_call_target="tpu_custom_call" | custom-call | tf_op jit(solution)/shard_map/experts_backward/pallas_call | solution.py:861
  182.4 26.5 %attention_backward.1 = (f32[320,512]{1,0:T(8,128)}, bf16[320,512]{1,0:T(8,128)(2,1)}, bf16[4,2,64,2176]{3,2,1,0:T(8,128)(2,1)}, bf16[4,4,16,2048]{3,2,1,0:T(8,128)(2,1)}, bf16[4,64,512]{2,1,0:T(8,128)(2,1)}) custom-call(f32[320,512]{1,0:T(8,128)} %get-tuple-element.80.refs_0_, f32[320,512]{1,0:T(8,128)} %get-tuple-element.81.refs_1_, ...), custom_call_target="tpu_custom_call" | custom-call | tf_op jit(solution)/shard_map/attention_backward/pallas_call | solution.py:1284
  208.9 68.2 %experts_backward_and_sums.1 = (f32[320,512]{1,0:T(8,128)}, f32[8,512]{1,0:T(8,128)}, bf16[4,512,256]{2,1,0:T(8,128)(2,1)}, bf16[1024,512]{1,0:T(8,128)(2,1)}, b...) custom-call(bf16[320,512]{1,0:T(8,128)(2,1)} %get-tuple-element.91.refs_0_, ...), custom_call_target="tpu_custom_call" | custom-call | tf_op jit(solution)/shard_map/experts_backward_and_sums/pallas_call | solution.py:861
  277.1 0.0 copy-start.4
  277.1 0.0 copy-start.8
  277.1 91.4 %attention_backward_last.1 = (f32[2,160,512]{2,1,0:T(8,128)}, bf16[2,160,512]{2,1,0:T(8,128)(2,1)}, bf16[4,2,64,2176]{3,2,1,0:T(8,128)(2,1)}, f32[2,64,1536]{2,1...) custom-call(f32[320,512]{1,0:T(8,128)} %get-tuple-element.90.refs_0_, ...), custom_call_target="tpu_custom_call" | custom-call | tf_op jit(solution)/shard_map/attention_backward_last/pallas_call | solution.py:1284
  368.5 0.0 copy-start.2
  368.5 1.9 slice_reduce_fusion
  370.4 0.9 slice.28
  371.3 0.7 copy.46
  372.0 0.0 copy-done.4
  372.0 0.0 copy-done.8
  372.0 0.1 pad_maximum_fusion
  372.1 0.0 copy-done.2
  372.1 0.0 copy-start
  372.1 0.0 copy-start.1
  372.1 2.3 maximum_convert_fusion.1
  374.4 0.0 copy-done
  374.4 0.0 copy-done.1
  374.5 0.0 copy-start.6
  374.5 0.0 copy-start.5
  374.5 2.3 maximum_convert_fusion
  376.8 0.0 copy-done.6
  376.8 0.0 copy-start.3
  376.8 0.0 copy-start.7
  376.8 0.7 copy.51
  377.5 0.0 copy-done.5
  377.5 0.8 copy.52
  378.3 0.0 copy-done.3
  378.3 0.9 copy.53
  379.2 0.0 copy-done.7
  379.2 0.7 copy.54
  (8 shorter events, 0.1 us)
Async XLA Ops:
  277.1 94.9 %copy-start.4 = (bf16[12,64,512]{2,1,0:T(8,128)(2,1)S(1)}, bf16[12,64,512]{2,1,0:T(8,128)(2,1)}, u32[]{:S(2)}) copy-start(bf16[12,64,512]{2,1,0:T(8,128)(2,1)} %get-tuple-element.116) | copy-start | bytes 2359300
  277.1 94.9 %copy-start.8 = (bf16[4,64,512]{2,1,0:T(8,128)(2,1)S(1)}, bf16[4,64,512]{2,1,0:T(8,128)(2,1)}, u32[]{:S(2)}) copy-start(bf16[4,64,512]{2,1,0:T(8,128)(2,1)} %get-tuple-element.115) | copy-start | bytes 786436
  368.5 3.6 copy-start.2
  372.1 2.3 copy-start
  372.1 2.3 copy-start.1
  374.5 2.3 copy-start.6
  374.5 3.0 copy-start.5
  376.8 1.6 copy-start.3
  376.8 2.5 copy-start.7

commit v2 on v1

--- a/solution.py
+++ b/solution.py
@@ -16,7 +16,7 @@
 VMEM_LIMIT = 60 * 1024 * 1024
 EXPERT_TICKS = ((0, 2, 1, 1, 1, 1, 1, 1), (1, 0, 1, 0), (1,), (1, 1, 0))
 HEAD_TICKS = ((0, 1, 1, 1), (1,), (1,))
-DENSE_TICKS = (5, 6, 14)
+DENSE_TICKS = (6, 7, 16)
 EARLY_CHUNKS = 4
 NT = ((1,), (1,))
 TN = ((0,), (0,))
@@ -693,11 +693,11 @@
         def tick(at):
             @pl.when(self.middle)
             def _():
-                for act, behind in ((self.relay, 0), (self.total, 1), (self.forward, 2)):
+                for act, behind in ((self.relay, 0), (self.total, 2), (self.forward, 4)):
                     if 0 <= at - behind < count:
                         act(*self.pairs[at - behind])
 
-        return [lambda at=at: tick(at) for at in range(count + 2)]
+        return [lambda at=at: tick(at) for at in range(count + 4)]
 
     def share_out(self, places):
         ticks, shared = self.ticks(), []
@@ -962,7 +962,8 @@
             keep_dense.start()
             dense_ref, chosen_ref = dense_all, chosen_all.at[level]
         else:
-            state_ref, dense_ref, chosen_ref, length_ref = taken
+            state_ref, dense_ref, chosen_all, length_ref = taken
+            chosen_ref = chosen_all.at[level]
             for r in range(1, size):
                 shift(r).start()
         rows_of = weight_rows(dense_ref)
@@ -1095,9 +1096,10 @@
 
 def attention_backward(
     grad, back, back_tail, state, middle, message, gates, chosen, queries, kv, log_total, mixed,
-    dense, length, up_grad, plan, job, last,
+    dense, length, up_grad, level, plan, job,
 ):
     rows, width = state.shape
+    last = level == 0
     share = plan.share
     keys_len = rows * share
     heads = width // HEAD
@@ -1122,7 +1124,9 @@
             up_ref, refs = refs[0], refs[1:]
         taken = len(job.args)
         job_refs, refs = refs[:taken], refs[taken:]
-        (new_ref, new_low_ref, dense_ref), refs = refs[:3], refs[3:]
+        (new_ref, new_low_ref), refs = refs[:2], refs[2:]
+        if not totals_shape:
+            dense_ref, refs = refs[0], refs[1:]
         if moved_out:
             moved_ref, refs = refs[0], refs[1:]
         if totals_shape:
@@ -1136,7 +1140,8 @@
             refs = refs[3:]
         if last:
             (pieces, piece_sem), refs = refs[:2], refs[2:]
-            if job.kinds:
+            if totals_shape:
+                dense_ref, refs = refs[0], refs[1:]
                 job_refs = (job_refs[0], moving[1], *job_refs[1:], dense_ref)
         summing = last and job.kinds
         job.bind(job_refs, job_outs, refs)
@@ -1156,7 +1161,7 @@
             job.dense_begin(job.dense[0])
         rows_of = weight_rows(weights)
         gates = gates_ref[...]
-        grad_gates = tail_ref[:, :rows] * chosen_ref[:, :rows]
+        grad_gates = tail_ref[:, :rows] * chosen_ref[level, :, :rows]
         grad_logits = split_rows(gates * (grad_gates - row_sums(gates * grad_gates)))
         router = jnp.concatenate([rows_of[4:8], jnp.zeros((4, width), F32)], 0)
         twice = jnp.concatenate([router, router], 0).astype(BF16)
@@ -1245,7 +1250,8 @@
         if last:
             for k in range(plan.images):
                 new_low_ref[k] = new[k * plan.piece : (k + 1) * plan.piece].astype(BF16)
-            swap.start(new_low_ref, pieces, piece_sem)
+            if not summing:
+                swap.start(new_low_ref, pieces, piece_sem)
         else:
             new_low_ref[...] = new.astype(BF16)
             new_ref[...] = new
@@ -1259,6 +1265,7 @@
                 job.dense_far(job.dense[0])
             if summing and at == DENSE_TICKS[2]:
                 job.dense_far(job.dense[1])
+                swap.start(new_low_ref, pieces, piece_sem)
             tick()
         job.finish()
         for at, kind in enumerate(job.kept):
@@ -1286,13 +1293,13 @@
         out_shape=(
             jax.ShapeDtypeStruct(image_shape, F32),
             jax.ShapeDtypeStruct(image_shape, BF16),
-            jax.ShapeDtypeStruct(dense_shape, BF16),
+            *([] if totals_shape else [jax.ShapeDtypeStruct(dense_shape, BF16)]),
             *([jax.ShapeDtypeStruct(shift.shape, BF16)] if moved_out else []),
             *totals_shape,
             *job.out_shape,
         ),
         in_specs=[in_vmem()] * (14 + moves + len(job.args)),
-        out_specs=(in_vmem(),) * (3 + moved_out + len(totals_shape)) + (in_any(),) * len(job.out_shape),
+        out_specs=(in_vmem(),) * (2 + (len(totals_shape) or 1) + moved_out) + (in_any(),) * len(job.out_shape),
         scratch_shapes=[
             pltpu.VMEM((width, keys_len), BF16),
             pltpu.VMEM((rows, width), BF16),
@@ -1307,6 +1314,7 @@
         ]
         + (shift.scratch_shapes if moves else [])
         + (last_scratch if last else [])
+        + ([pltpu.VMEM(dense_shape, BF16)] if totals_shape else [])
         + job.scratch_shapes,
         compiler_params=pltpu.CompilerParams(
             collective_id=9 if last else 8, has_side_effects=True, vmem_limit_bytes=VMEM_LIMIT
@@ -1361,7 +1369,7 @@
         for level in range(levels):
             if level:
                 made = attention_forward(
-                    plan, level, expert_in, later=(state, dense, chosen[level], length)
+                    plan, level, expert_in, later=(state, dense, chosen, length)
                 )
             else:
                 *made, grad, grad_low, state, chosen, length, dense = attention_forward(
@@ -1372,7 +1380,7 @@
                 message, middle, up, down_all, level, plan.dp, strips if level + 1 < levels else ()
             )
             attended = (
-                state, middle, message, gates, chosen[level], queries, kv, log_total, mixed,
+                state, middle, message, gates, chosen, queries, kv, log_total, mixed,
                 dense, length,
             )
             dense = next_dense[0] if next_dense else None
@@ -1406,9 +1414,11 @@
                     dense_more=dense_grad,
                     dense=jax.ShapeDtypeStruct(dense_grad.shape, BF16),
                 )
-            grad, grad_low, dense_grad, *others = attention_backward(
-                grad, back, back_tail, *attended, up_grad if lined else None, plan, job, last
+            grad, grad_low, *others = attention_backward(
+                grad, back, back_tail, *attended, up_grad if lined else None, level, plan, job
             )
+            if not (lined and last):
+                dense_grad, *others = others
             if not lined:
                 sums[level] = sum_weights_plainly(plan.dp, down_grad, up_grad, dense_grad)
             elif last:

time: 381 us -> 375 us (0.984)
  Pallas kernels: 362 us -> 358 us
where the time goes in v2:
time: 375 us; the launch traced here: 374 us
  Pallas kernels  358 us (95%)
  local copies, waits for them, and re-layouts  8.52 us (2%)
  other arithmetic  6.95 us (2%)
    pallas_call x2, Pallas kernels, attention_backward(): pl.pallas_call(kernel, out_shape=(jax.ShapeDtypeStruct(image_shape, F32),...  116 us
    pallas_call x2, Pallas kernels, experts_backward(): pl.pallas_call(kernel, out_shape=(jax.ShapeDtypeStruct((rows, width), F32...  105 us
    pallas_call x2, Pallas kernels, experts_forward(): pl.pallas_call(kernel, out_shape=(jax.ShapeDtypeStruct((rows, width), F32...  82.8 us
    pallas_call x2, Pallas kernels, attention_forward(): pl.pallas_call(kernel, out_shape=(jax.ShapeDtypeStruct((rows + 16, width)...  54.2 us

profile of v2, /device:TPU:0, one launch (start us, length us, event | category | flops | bytes accessed | tf_op | source)
XLA Modules:
  0.0 374.3 jit_solution(5741604052934308651)
XLA Ops:
  0.7 0.8 reduce_sum.19
  1.5 0.1 copy.40
  1.6 0.1 add_convert_fusion
  1.7 0.1 mul.22
  1.8 0.1 mul.23
  1.8 0.7 convert_reduce_fusion
  2.6 0.1 mul.21
  2.7 0.1 broadcast_in_dim.17
  2.8 0.6 pad_maximum_fusion.1.refs_1_
  3.4 1.4 copy.44.refs_5_.refs_2_
  4.8 35.2 %attention_forward_first.1 = (bf16[336,512]{1,0:T(8,128)(2,1)}, f32[320,512]{1,0:T(8,128)}, bf16[320,512]{1,0:T(8,128)(2,1)}, bf16[2,320,1024]{2,1,0:T(8,128)(2,...) custom-call(bf16[2,4,64,2048]{3,2,1,0:T(8,128)(2,1)} %in_ref.3, ...), custom_call_target="tpu_custom_call" | custom-call | tf_op jit(solution)/shard_map/attention_forward_first/pallas_call | solution.py:1062
  40.1 43.6 %experts_forward.2 = (f32[320,512]{1,0:T(8,128)}, bf16[320,512]{1,0:T(8,128)(2,1)}, bf16[8,336,512]{2,1,0:T(8,128)(2,1)}, bf16[8,320,1024]{2,1,0:T(8,128)(2,1)},...) custom-call(bf16[336,512]{1,0:T(8,128)(2,1)} %get-tuple-element.65.msg_ref.refs_5_, ...), custom_call_target="tpu_custom_call" | custom-call | tf_op jit(solution)/shard_map/experts_forward/pallas_call | solution.py:465
  83.7 19.0 %attention_forward.1 = (bf16[336,512]{1,0:T(8,128)(2,1)}, f32[320,512]{1,0:T(8,128)}, bf16[320,512]{1,0:T(8,128)(2,1)}, bf16[2,320,1024]{2,1,0:T(8,128)(2,1)}, f...) custom-call(bf16[2,4,64,2048]{3,2,1,0:T(8,128)(2,1)} %in_ref.3, ...), custom_call_target="tpu_custom_call" | custom-call | tf_op jit(solution)/shard_map/attention_forward/pallas_call | solution.py:1062
  102.6 39.2 %experts_forward.3 = (f32[320,512]{1,0:T(8,128)}, bf16[320,512]{1,0:T(8,128)(2,1)}, bf16[8,336,512]{2,1,0:T(8,128)(2,1)}, bf16[8,320,1024]{2,1,0:T(8,128)(2,1)}, bf16[8,320,1024]{2,1,0:T(8,128)(2,1)}) custom-call(bf16[336,512]{1,0:T(8,128)(2,1)} %get-tuple-element.72.msg_ref.refs_5_, f32[320,512]{1,0:T(8,128)} %get-tuple-element.73.mid_ref.refs_4_, ...), custom_call_target="tpu_custom_call" | custom-call | tf_op jit(solution)/shard_map/experts_forward/pallas_call | solution.py:465
  141.9 39.1 %experts_backward.1 = (f32[320,512]{1,0:T(8,128)}, f32[8,512]{1,0:T(8,128)}, bf16[4,512,256]{2,1,0:T(8,128)(2,1)}, bf16[1024,512]{1,0:T(8,128)(2,1)}, bf16[2,160,512]{2,1,0:T(8,128)(2,1)}) custom-call(bf16[320,512]{1,0:T(8,128)(2,1)} %get-tuple-element.64.refs_0_, bf16[8,336,512]{2,1,0:T(8,128)(2,1)} %get-tuple-element.75.refs_1_, ...), custom_call_target="tpu_custom_call" | custom-call | tf_op jit(solution)/shard_map/experts_backward/pallas_call | solution.py:861
  181.0 26.2 %attention_backward.1 = (f32[320,512]{1,0:T(8,128)}, bf16[320,512]{1,0:T(8,128)(2,1)}, bf16[4,2,64,2176]{3,2,1,0:T(8,128)(2,1)}, bf16[4,4,16,2048]{3,2,1,0:T(8,128)(2,1)}, bf16[4,64,512]{2,1,0:T(8,128)(2,1)}) custom-call(f32[320,512]{1,0:T(8,128)} %get-tuple-element.80.refs_0_, f32[320,512]{1,0:T(8,128)} %get-tuple-element.81.refs_1_, ...), custom_call_target="tpu_custom_call" | custom-call | tf_op jit(solution)/shard_map/attention_backward/pallas_call | solution.py:1291
  207.2 65.7 %experts_backward_and_sums.1 = (f32[320,512]{1,0:T(8,128)}, f32[8,512]{1,0:T(8,128)}, bf16[4,512,256]{2,1,0:T(8,128)(2,1)}, bf16[1024,512]{1,0:T(8,128)(2,1)}, b...) custom-call(bf16[320,512]{1,0:T(8,128)(2,1)} %get-tuple-element.91.refs_0_, ...), custom_call_target="tpu_custom_call" | custom-call | tf_op jit(solution)/shard_map/experts_backward_and_sums/pallas_call | solution.py:861
  272.9 0.0 copy-start.4
  273.0 0.0 copy-start.8
  273.0 89.9 %attention_backward_last.1 = (f32[2,160,512]{2,1,0:T(8,128)}, bf16[2,160,512]{2,1,0:T(8,128)(2,1)}, f32[2,64,1536]{2,1,0:T(8,128)}, f32[2,64,512]{2,1,0:T(8,128)...) custom-call(f32[320,512]{1,0:T(8,128)} %get-tuple-element.90.refs_0_, ...), custom_call_target="tpu_custom_call" | custom-call | tf_op jit(solution)/shard_map/attention_backward_last/pallas_call | solution.py:1291
  362.9 0.0 copy-start.2
  362.9 1.8 slice_reduce_fusion
  364.8 0.9 slice.19
  365.7 0.7 copy.46
  366.4 0.0 copy-done.4
  366.4 0.0 copy-done.8
  366.4 0.1 pad_maximum_fusion
  366.5 0.0 copy-done.2
  366.5 0.0 copy-start
  366.5 0.0 copy-start.1
  366.5 2.3 maximum_convert_fusion.1
  368.8 0.0 copy-done
  368.8 0.0 copy-done.1
  368.8 0.0 copy-start.6
  368.8 0.0 copy-start.5
  368.8 2.3 maximum_convert_fusion
  371.1 0.0 copy-done.6
  371.1 0.0 copy-start.3
  371.1 0.0 copy-start.7
  371.1 0.7 copy.51
  371.8 0.0 copy-done.5
  371.8 0.8 copy.52
  372.7 0.0 copy-done.3
  372.7 0.9 copy.53
  373.6 0.0 copy-done.7
  373.6 0.7 copy.54
  (8 shorter events, 0.1 us)
Async XLA Ops:
  272.9 93.4 %copy-start.4 = (bf16[12,64,512]{2,1,0:T(8,128)(2,1)S(1)}, bf16[12,64,512]{2,1,0:T(8,128)(2,1)}, u32[]{:S(2)}) copy-start(bf16[12,64,512]{2,1,0:T(8,128)(2,1)} %get-tuple-element.116) | copy-start | bytes 2359300
  273.0 93.4 %copy-start.8 = (bf16[4,64,512]{2,1,0:T(8,128)(2,1)S(1)}, bf16[4,64,512]{2,1,0:T(8,128)(2,1)}, u32[]{:S(2)}) copy-start(bf16[4,64,512]{2,1,0:T(8,128)(2,1)} %get-tuple-element.115) | copy-start | bytes 786436
  362.9 3.6 copy-start.2
  366.5 2.3 copy-start
  366.5 2.3 copy-start.1
  368.8 2.3 copy-start.6
  368.8 3.0 copy-start.5
  371.1 1.6 copy-start.3
  371.1 2.5 copy-start.7

commit v3 on v2

--- a/solution.py
+++ b/solution.py
@@ -14,7 +14,7 @@
 BF16 = jnp.bfloat16
 MESH = pl.DeviceIdType.MESH
 VMEM_LIMIT = 60 * 1024 * 1024
-EXPERT_TICKS = ((0, 2, 1, 1, 1, 1, 1, 1), (1, 0, 1, 0), (1,), (1, 1, 0))
+EXPERT_TICKS = ((0, 2, 1, 1, 1, 1, 1, 1), (1, 1, 1, 1), (1,), (2, 2, 1))
 HEAD_TICKS = ((0, 1, 1, 1), (1,), (1,))
 DENSE_TICKS = (6, 7, 16)
 EARLY_CHUNKS = 4
@@ -79,7 +79,9 @@
 
 def gelu_parts(u):
     bell = jnp.exp2(u * u * -0.7213475204444817)
-    t = pl.reciprocal(1.0 + 0.23164190 * jnp.abs(u), approx=True)
+    under = 1.0 + 0.23164190 * jnp.abs(u)
+    t = pl.reciprocal(under, approx=True)
+    t = t * (2.0 - under * t)
     poly = t * (
         0.127414796 + t * (-0.142248368 + t * (0.7107068705 + t * (-0.7265760135 + t * 0.5307027145)))
     )

time: 375 us -> 375 us (level)
  no operation moved by 1% of the time
where the time goes in v3:
time: 375 us
  Pallas kernels  358 us (95%)
  local copies, waits for them, and re-layouts  8.52 us (2%)
  other arithmetic  6.95 us (2%)
    pallas_call x2, Pallas kernels, attention_backward(): pl.pallas_call(kernel, out_shape=(jax.ShapeDtypeStruct(image_shape, F32),...  116 us
    pallas_call x2, Pallas kernels, experts_backward(): pl.pallas_call(kernel, out_shape=(jax.ShapeDtypeStruct((rows, width), F32...  105 us
    pallas_call x2, Pallas kernels, experts_forward(): pl.pallas_call(kernel, out_shape=(jax.ShapeDtypeStruct((rows, width), F32...  83.1 us
    pallas_call x2, Pallas kernels, attention_forward(): pl.pallas_call(kernel, out_shape=(jax.ShapeDtypeStruct((rows + 16, width)...  54.2 us

profile of v3, /device:TPU:0, one launch (start us, length us, event | category | flops | bytes accessed | tf_op | source)
XLA Modules:
  0.0 374.6 jit_solution(7600674142544187924)
XLA Ops:
  0.7 0.8 reduce_sum.19
  1.5 0.1 copy.40
  1.6 0.1 add_convert_fusion
  1.7 0.1 mul.22
  1.8 0.1 mul.23
  1.8 0.7 convert_reduce_fusion
  2.6 0.1 mul.21
  2.7 0.1 broadcast_in_dim.17
  2.8 0.6 pad_maximum_fusion.1.refs_1_
  3.4 1.4 copy.44.refs_5_.refs_2_
  4.8 35.2 %attention_forward_first.1 = (bf16[336,512]{1,0:T(8,128)(2,1)}, f32[320,512]{1,0:T(8,128)}, bf16[320,512]{1,0:T(8,128)(2,1)}, bf16[2,320,1024]{2,1,0:T(8,128)(2,...) custom-call(bf16[2,4,64,2048]{3,2,1,0:T(8,128)(2,1)} %in_ref.3, ...), custom_call_target="tpu_custom_call" | custom-call | tf_op jit(solution)/shard_map/attention_forward_first/pallas_call | solution.py:1064
  40.1 43.6 %experts_forward.2 = (f32[320,512]{1,0:T(8,128)}, bf16[320,512]{1,0:T(8,128)(2,1)}, bf16[8,336,512]{2,1,0:T(8,128)(2,1)}, bf16[8,320,1024]{2,1,0:T(8,128)(2,1)},...) custom-call(bf16[336,512]{1,0:T(8,128)(2,1)} %get-tuple-element.65.msg_ref.refs_5_, ...), custom_call_target="tpu_custom_call" | custom-call | tf_op jit(solution)/shard_map/experts_forward/pallas_call | solution.py:467
  83.7 19.0 %attention_forward.1 = (bf16[336,512]{1,0:T(8,128)(2,1)}, f32[320,512]{1,0:T(8,128)}, bf16[320,512]{1,0:T(8,128)(2,1)}, bf16[2,320,1024]{2,1,0:T(8,128)(2,1)}, f...) custom-call(bf16[2,4,64,2048]{3,2,1,0:T(8,128)(2,1)} %in_ref.3, ...), custom_call_target="tpu_custom_call" | custom-call | tf_op jit(solution)/shard_map/attention_forward/pallas_call | solution.py:1064
  102.6 39.6 %experts_forward.3 = (f32[320,512]{1,0:T(8,128)}, bf16[320,512]{1,0:T(8,128)(2,1)}, bf16[8,336,512]{2,1,0:T(8,128)(2,1)}, bf16[8,320,1024]{2,1,0:T(8,128)(2,1)}, bf16[8,320,1024]{2,1,0:T(8,128)(2,1)}) custom-call(bf16[336,512]{1,0:T(8,128)(2,1)} %get-tuple-element.72.msg_ref.refs_5_, f32[320,512]{1,0:T(8,128)} %get-tuple-element.73.mid_ref.refs_4_, ...), custom_call_target="tpu_custom_call" | custom-call | tf_op jit(solution)/shard_map/experts_forward/pallas_call | solution.py:467
  142.2 39.1 %experts_backward.1 = (f32[320,512]{1,0:T(8,128)}, f32[8,512]{1,0:T(8,128)}, bf16[4,512,256]{2,1,0:T(8,128)(2,1)}, bf16[1024,512]{1,0:T(8,128)(2,1)}, bf16[2,160,512]{2,1,0:T(8,128)(2,1)}) custom-call(bf16[320,512]{1,0:T(8,128)(2,1)} %get-tuple-element.64.refs_0_, bf16[8,336,512]{2,1,0:T(8,128)(2,1)} %get-tuple-element.75.refs_1_, ...), custom_call_target="tpu_custom_call" | custom-call | tf_op jit(solution)/shard_map/experts_backward/pallas_call | solution.py:863
  181.3 26.4 %attention_backward.1 = (f32[320,512]{1,0:T(8,128)}, bf16[320,512]{1,0:T(8,128)(2,1)}, bf16[4,2,64,2176]{3,2,1,0:T(8,128)(2,1)}, bf16[4,4,16,2048]{3,2,1,0:T(8,128)(2,1)}, bf16[4,64,512]{2,1,0:T(8,128)(2,1)}) custom-call(f32[320,512]{1,0:T(8,128)} %get-tuple-element.80.refs_0_, f32[320,512]{1,0:T(8,128)} %get-tuple-element.81.refs_1_, ...), custom_call_target="tpu_custom_call" | custom-call | tf_op jit(solution)/shard_map/attention_backward/pallas_call | solution.py:1293
  207.7 65.6 %experts_backward_and_sums.1 = (f32[320,512]{1,0:T(8,128)}, f32[8,512]{1,0:T(8,128)}, bf16[4,512,256]{2,1,0:T(8,128)(2,1)}, bf16[1024,512]{1,0:T(8,128)(2,1)}, b...) custom-call(bf16[320,512]{1,0:T(8,128)(2,1)} %get-tuple-element.91.refs_0_, ...), custom_call_target="tpu_custom_call" | custom-call | tf_op jit(solution)/shard_map/experts_backward_and_sums/pallas_call | solution.py:863
  273.3 0.0 copy-start.4
  273.3 0.0 copy-start.8
  273.3 89.9 %attention_backward_last.1 = (f32[2,160,512]{2,1,0:T(8,128)}, bf16[2,160,512]{2,1,0:T(8,128)(2,1)}, f32[2,64,1536]{2,1,0:T(8,128)}, f32[2,64,512]{2,1,0:T(8,128)...) custom-call(f32[320,512]{1,0:T(8,128)} %get-tuple-element.90.refs_0_, ...), custom_call_target="tpu_custom_call" | custom-call | tf_op jit(solution)/shard_map/attention_backward_last/pallas_call | solution.py:1293
  363.2 0.0 copy-start.2
  363.2 1.8 slice_reduce_fusion
  365.1 0.9 slice.19
  366.0 0.7 copy.46
  366.7 0.0 copy-done.4
  366.7 0.0 copy-done.8
  366.7 0.1 pad_maximum_fusion
  366.8 0.0 copy-done.2
  366.8 0.0 copy-start
  366.8 0.0 copy-start.1
  366.8 2.3 maximum_convert_fusion.1
  369.1 0.0 copy-done
  369.1 0.0 copy-done.1
  369.2 0.0 copy-start.6
  369.2 0.0 copy-start.5
  369.2 2.3 maximum_convert_fusion
  371.4 0.0 copy-done.6
  371.4 0.0 copy-start.3
  371.5 0.0 copy-start.7
  371.5 0.7 copy.51
  372.2 0.0 copy-done.5
  372.2 0.8 copy.52
  373.0 0.0 copy-done.3
  373.0 0.9 copy.53
  373.9 0.0 copy-done.7
  373.9 0.7 copy.54
  (8 shorter events, 0.1 us)
Async XLA Ops:
  273.3 93.4 %copy-start.4 = (bf16[12,64,512]{2,1,0:T(8,128)(2,1)S(1)}, bf16[12,64,512]{2,1,0:T(8,128)(2,1)}, u32[]{:S(2)}) copy-start(bf16[12,64,512]{2,1,0:T(8,128)(2,1)} %get-tuple-element.116) | copy-start | bytes 2359300
  273.3 93.4 %copy-start.8 = (bf16[4,64,512]{2,1,0:T(8,128)(2,1)S(1)}, bf16[4,64,512]{2,1,0:T(8,128)(2,1)}, u32[]{:S(2)}) copy-start(bf16[4,64,512]{2,1,0:T(8,128)(2,1)} %get-tuple-element.115) | copy-start | bytes 786436
  363.2 3.6 copy-start.2
  366.8 2.3 copy-start
  366.8 2.3 copy-start.1
  369.2 2.3 copy-start.6
  369.2 3.0 copy-start.5
  371.4 1.6 copy-start.3
  371.5 2.5 copy-start.7
